TPU v7x, 256 devices: a whole 4x4x8 slice. The times are simulated.
256 devices in a mesh: gx: 4 (over z_hi, core), yz: 64 (over x, z_lo, y).
Axes of the slice: x: 4, y: 4, z: 8 (z_hi: 2, z_lo: 4; z = z_hi * 4 + z_lo), core: 2. Of those that a mesh axis runs over, the one named last changes fastest.
Arguments:
- hidden_in: bfloat16 [2, 256, 9216], P(None, 'yz', 'gx'), may hold values from -80 to 80
- norm_gain: float32 [9216], P('gx'), may hold values from 0.5 to 1.5
- w_qkv: bfloat16 [9216, 6656], P('gx', 'yz'), may hold values from -0.0625 to 0.0625
- w_gate: bfloat16 [9216, 36864], P('gx', 'yz'), may hold values from -0.0625 to 0.0625
- w_up: bfloat16 [9216, 36864], P('gx', 'yz'), may hold values from -0.0625 to 0.0625
- w_out: bfloat16 [6144, 9216], P('yz', 'gx'), may hold values from -0.078125 to 0.078125
- w_down: bfloat16 [36864, 9216], P('yz', 'gx'), may hold values from -0.03125 to 0.03125
- kv_cache: bfloat16 [256, 2048, 512], P(('gx', 'yz')), may hold values from -304 to 304
- lengths: int32 [256], P(('gx', 'yz')), may hold values from 1 to 2048, as said below
Outputs:
- layer_out: bfloat16 [2, 256, 9216], P(None, 'yz', 'gx')
Inputs may be any that keep to these rules, and one draw needn't show every extreme that they name: `lengths`: every row has 1 to 2048 cached tokens; some row has exactly 2048 and some exactly 1.
All inputs are finite; a program needn't handle non-finite values.
Results may differ from a plain program's by a relative error of at most 0.009.
Values may be sent and summed in bfloat16 or wider, within the bound.
A program may use at most 64 MiB of HBM per device.

v0:
```python
import jax
import jax.numpy as jnp
from jax import lax
from jax.sharding import PartitionSpec as P

D = 9216
HEADS = 24
HEAD_DIM = 256
CTX = 2048
STEPS = 2


EPS = 1e-06
SCALE = 0.0625


def rotate(values, position):
    half = values.shape[-1] // 2
    freqs = 10000.0 ** (-jnp.arange(half, dtype=jnp.float32) / half)
    angle = position[..., None] * freqs
    cosine = jnp.cos(angle)
    sine = jnp.sin(angle)
    first = values[..., :half]
    second = values[..., half:]
    return jnp.concatenate([first * cosine - second * sine, second * cosine + first * sine], -1)


def attend(queries, kv_cache, lengths, keys_new, values_new):
    local_rows = queries.shape[0]
    cached_keys = kv_cache[:, :, :HEAD_DIM]
    cached_values = kv_cache[:, :, HEAD_DIM:]
    old_scores = (
        jnp.einsum("bhd,btd->bht", queries, cached_keys, preferred_element_type=jnp.float32) * SCALE
    )
    valid = jnp.arange(CTX)[None, None, :] < lengths[:, None, None]
    old_scores = jnp.where(valid, old_scores, jnp.float32(-1e30))
    new_scores = (
        jnp.einsum("bhd,bnd->bhn", queries, keys_new, preferred_element_type=jnp.float32) * SCALE
    )
    scores = jnp.concatenate([old_scores, new_scores], 2)
    peak = jnp.max(scores, 2, keepdims=True)
    expd = jnp.exp(scores - peak)
    weights = (expd / jnp.sum(expd, 2, keepdims=True)).astype(jnp.bfloat16)
    mixed = jnp.einsum(
        "bht,btd->bhd", weights[:, :, :CTX], cached_values, preferred_element_type=jnp.float32
    )
    mixed = mixed + jnp.einsum(
        "bhn,bnd->bhd", weights[:, :, CTX:], values_new, preferred_element_type=jnp.float32
    )
    return mixed.reshape(local_rows, HEADS * HEAD_DIM).astype(jnp.bfloat16)


def per_device(hidden_in, norm_gain, w_qkv, w_gate, w_up, w_out, w_down, kv_cache, lengths):
    outputs = []
    keys_list = []
    values_list = []
    for step in range(STEPS):
        layer_in = hidden_in[step]
        values_f = layer_in.astype(jnp.float32)
        sums, squares = lax.psum((jnp.sum(values_f, 1), jnp.sum(values_f * values_f, 1)), "gx")
        mean = sums / D
        var = squares / D - mean * mean
        normed = ((values_f - mean[:, None]) * lax.rsqrt(var[:, None] + EPS) * norm_gain).astype(
            jnp.bfloat16
        )
        every_row = lax.all_gather(normed, "yz", axis=0, tiled=True)
        qkv_share = lax.psum_scatter(
            jnp.dot(every_row, w_qkv, preferred_element_type=jnp.float32).astype(jnp.bfloat16),
            "gx",
            scatter_dimension=0,
            tiled=True,
        )
        row_qkv = lax.all_to_all(qkv_share, "yz", split_axis=0, concat_axis=1, tiled=True)
        position = lengths.astype(jnp.float32) + step
        query_part = row_qkv[:, : HEADS * HEAD_DIM].reshape(-1, HEADS, HEAD_DIM).astype(jnp.float32)
        queries = rotate(query_part, position[:, None]).astype(jnp.bfloat16)
        key_part = row_qkv[:, HEADS * HEAD_DIM : (HEADS + 1) * HEAD_DIM].astype(jnp.float32)
        keys_list.append(rotate(key_part, position).astype(jnp.bfloat16))
        values_list.append(row_qkv[:, (HEADS + 1) * HEAD_DIM :])
        attended = attend(
            queries, kv_cache, lengths, jnp.stack(keys_list, 1), jnp.stack(values_list, 1)
        )
        head_block = lax.all_to_all(attended, "yz", split_axis=1, concat_axis=0, tiled=True)
        head_rows = lax.all_gather(head_block, "gx", axis=0, tiled=True)
        gate_part, up_part = lax.psum(
            (
                jnp.dot(every_row, w_gate, preferred_element_type=jnp.float32),
                jnp.dot(every_row, w_up, preferred_element_type=jnp.float32),
            ),
            "gx",
        )
        hidden = (jax.nn.silu(gate_part) * up_part).astype(jnp.bfloat16)
        attn_sum = lax.psum_scatter(
            jnp.dot(head_rows, w_out, preferred_element_type=jnp.float32),
            "yz",
            scatter_dimension=0,
            tiled=True,
        )
        ffn_sum = lax.psum_scatter(
            jnp.dot(hidden, w_down, preferred_element_type=jnp.float32),
            "yz",
            scatter_dimension=0,
            tiled=True,
        )
        total = attn_sum + ffn_sum
        outputs.append((values_f + total).astype(jnp.bfloat16))
    return jnp.stack(outputs)


def solution(mesh):
    return jax.shard_map(
        per_device,
        mesh=mesh,
        in_specs=(
            P(None, "yz", "gx"),
            P("gx"),
            P("gx", "yz"),
            P("gx", "yz"),
            P("gx", "yz"),
            P("yz", "gx"),
            P("yz", "gx"),
            P(("gx", "yz"), None, None),
            P(("gx", "yz")),
        ),
        out_specs=P(None, "yz", "gx"),
        check_vma=False,
    )
```

profile of v0, /device:TPU:2, one launch (start us, length us, event | category | flops | bytes accessed | tf_op | source)
XLA Modules:
  0.0 1607.5 jit_solution(8449539859970283302)
XLA Ops:
  8.5 16.5 %all-reduce.3 = (f32[4]{0:T(128)S(1)}, f32[4]{0:T(128)S(1)}, f32[4]{0:T(128)S(1)}, f32[4]{0:T(128)S(1)}) all-reduce(f32[4]{0:T(128)S(1)} %get-tuple-element.8, f32[4]{0:T(128)S(1)} %get-tuple-element.6, f32[4]{0:T(128)S(1)} %get-tuple-element.7, f32[4]{0:T(128)S(1)} %get-tuple-element.5), channel_id=1, replica_groups=mesh['gx'=4,'yz'=64] {'gx'}, use_global_device_ids=true, to_apply=%region_14.15 | all-reduce | flops 16 | bytes 128 | tf_op jit(solution)/shard_map/psum | solution.py:60
  28.1 309.3 %all-gather.7.cloned.1.call-done = bf16[64,4,2304]{2,1,0:T(4,128)(2,1)} async-done(((bf16[1,4,2304]{2,1,0:T(4,128)(2,1)}), bf16[64,4,2304]{2,1,0:T(4,128)(2,1)}) %all-gather.7.cloned.1.call-update) | async-done | bytes 1179664 | tf_op jit(solution)/shard_map/all_gather | solution.py:66
  337.4 3.1 reshape.644
  340.4 2.3 convolution_convert_fusion.1
  342.8 4.0 fusion.69
  348.5 336.1 %all-gather.9.cloned.1.call-done = bf16[64,4,2304]{2,1,0:T(4,128)(2,1)} async-done(((bf16[1,4,2304]{2,1,0:T(4,128)(2,1)}), bf16[64,4,2304]{2,1,0:T(4,128)(2,1)}) %all-gather.9.cloned.1.call-update) | async-done | bytes 1179664 | tf_op jit(solution)/shard_map/all_gather | solution.py:66
  684.6 3.1 reshape.646
  687.7 3.9 fusion.71
  692.7 61.3 %reduce-scatter.3.cloned.1.call-done = bf16[64,104]{1,0:T(8,128)(2,1)} async-done(((bf16[256,104]{1,0:T(8,128)(2,1)}), bf16[64,104]{1,0:T(8,128)(2,1)}) %reduce-scatter.3.cloned.1.call-update) | async-done | bytes 13328 | tf_op jit(solution)/shard_map/reduce_scatter | solution.py:67
  755.4 8.2 all-to-all-start
  763.7 3.9 fusion.72
  767.6 20.0 %reduce-scatter.5.cloned.1.call-done = bf16[64,104]{1,0:T(8,128)(2,1)} async-done(((bf16[256,104]{1,0:T(8,128)(2,1)}), bf16[64,104]{1,0:T(8,128)(2,1)}) %reduce-scatter.5.cloned.1.call-update) | async-done | bytes 13328 | tf_op jit(solution)/shard_map/reduce_scatter | solution.py:67
  788.9 8.2 all-to-all-start.2
  797.5 9.1 all-to-all-done.2
  811.6 19.6 %all-to-all-start.1 = ((bf16[1,64,96]{2,0,1:T(2,128)(2,1)}), bf16[1,64,96]{2,0,1:T(2,128)(2,1)S(1)}, u32[]{:S(2)}, u32[]{:S(2)}) async-start(bf16[1,64,96]{2,0,1:T(2,128)(2,1)} %convert_element_type.184), calls=%async_computation.2 | async-start | bytes 65536 | tf_op jit(solution)/shard_map/all_to_all | solution.py:83
  836.0 4.9 all-to-all-done.1
  840.9 5.8 all-to-all-start.3
  846.7 9.0 all-to-all-done.3
  855.7 14.5 all-gather
  870.2 10.4 all-gather.1
  884.4 14.3 all-reduce.10.cloned.1.call-done
  898.7 4.7 convolution_add_fusion.1
  903.4 2.7 convolution_add_fusion
  908.0 691.0 %all-reduce.8.cloned.1.call-done = (f32[256,2304]{1,0:T(8,128)}, f32[256,2304]{1,0:T(8,128)}) async-done(((f32[256,2304]{1,0:T(8,128)}, f32[256,2304]{1,0:T(8,128)}), (f32[256,2304]{1,0:T(8,128)}, f32[256,2304]{1,0:T(8,128)})) %all-reduce.8.cloned.1.call-update) | async-done | bytes 4718608
  (88 shorter events, 26.6 us)
Async XLA Ops:
  6.5 892.2 %copy-start = (bf16[576,2304]{1,0:T(8,128)(2,1)S(1)}, bf16[576,2304]{1,0:T(8,128)(2,1)}, u32[]{:S(2)}) copy-start(bf16[576,2304]{1,0:T(8,128)(2,1)} %param.15) | copy-start | bytes 7962628
  6.5 333.9 %copy-start.4 = (bf16[2304,104]{0,1:T(8,128)(2,1)S(1)}, bf16[2304,104]{0,1:T(8,128)(2,1)}, u32[]{:S(2)}) copy-start(bf16[2304,104]{0,1:T(8,128)(2,1)} %param.11) | copy-start | bytes 1437700
  6.5 330.8 %all-gather.7.cloned.1.call-start = ((), (), s32[]{:S(2)}) async-start(), calls=%async_computation.8 | async-start | bytes 1198080 | tf_op jit(solution)/shard_map/all_gather | solution.py:66
  26.5 658.1 %all-gather.9.cloned.1.call-start = ((), (), s32[]{:S(2)}) async-start(), calls=%async_computation.9 | async-start | bytes 1198080 | tf_op jit(solution)/shard_map/all_gather | solution.py:66
  27.3 726.8 %reduce-scatter.3.cloned.1.call-start = ((), (), s32[]{:S(2)}) async-start(), calls=%async_computation.6 | async-start | bytes 81920 | tf_op jit(solution)/shard_map/reduce_scatter | solution.py:67
  342.8 4.0 copy-start.3
  342.8 4.0 copy-start.9
  348.5 439.1 %reduce-scatter.5.cloned.1.call-start = ((), (), s32[]{:S(2)}) async-start(), calls=%async_computation.7 | async-start | bytes 81920 | tf_op jit(solution)/shard_map/reduce_scatter | solution.py:67
  687.7 3.9 copy-start.2
  755.4 33.5 %all-to-all-start = ((bf16[64,1,104]{2,1,0:T(2,128)(2,1)}), bf16[64,1,104]{2,1,0:T(2,128)(2,1)S(1)}, u32[]{:S(2)}, u32[]{:S(2)}) async-start(bf16[64,1,104]{2,1,0:T(2,128)(2,1)} %copy.32), calls=%async_computation.1 | async-start | bytes 65536 | tf_op jit(solution)/shard_map/all_to_all | solution.py:73
  763.6 135.1 %all-reduce.10.cloned.1.call-start = ((), (), s32[]{:S(2)}) async-start(), calls=%async_computation.11 | async-start | bytes 4718592 | tf_op jit(solution)/shard_map/psum | solution.py:85
  788.9 17.6 %all-to-all-start.2 = ((bf16[64,1,104]{2,1,0:T(2,128)(2,1)}), bf16[64,1,104]{2,1,0:T(2,128)(2,1)S(1)}, u32[]{:S(2)}, u32[]{:S(2)}) async-start(bf16[64,1,104]{2,1,0:T(2,128)(2,1)} %copy.37), calls=%async_computation.4 | async-start | bytes 65536 | tf_op jit(solution)/shard_map/all_to_all | solution.py:73
  809.4 71.2 %copy-start.5 = (bf16[96,2304]{1,0:T(8,128)(2,1)S(1)}, bf16[96,2304]{1,0:T(8,128)(2,1)}, u32[]{:S(2)}) copy-start(bf16[96,2304]{1,0:T(8,128)(2,1)} %param.14) | copy-start | bytes 1327108
  811.6 29.2 %all-to-all-start.1 = ((bf16[1,64,96]{2,0,1:T(2,128)(2,1)}), bf16[1,64,96]{2,0,1:T(2,128)(2,1)S(1)}, u32[]{:S(2)}, u32[]{:S(2)}) async-start(bf16[1,64,96]{2,0,1:T(2,128)(2,1)} %convert_element_type.184), calls=%async_computation.2 | async-start | bytes 65536 | tf_op jit(solution)/shard_map/all_to_all | solution.py:83
  840.9 14.8 all-to-all-start.3
  846.6 752.4 %all-reduce.8.cloned.1.call-start = ((), (), s32[]{:S(2)}) async-start(), calls=%async_computation.10 | async-start | bytes 9437184
  898.7 4.7 copy-start.1
  898.7 4.7 copy-start.6
  898.7 4.7 copy-start.7
  906.1 0.7 copy-start.11
  906.1 693.0 %copy-start.8 = (bf16[2,4,2304]{2,1,0:T(4,128)(2,1)S(1)}, bf16[2,4,2304]{2,1,0:T(4,128)(2,1)}, u32[]{:S(2)}) copy-start(bf16[2,4,2304]{2,1,0:T(4,128)(2,1)} %param.9) | copy-start | bytes 110596
  1600.0 0.6 copy-start.10
Sparse Core Ops, SparseCore 0:
  26.6 310.6 all-gather.6
  339.1 345.4 all-gather.8
  687.3 66.7 reduce-scatter.2
  756.8 30.7 reduce-scatter.4
  790.3 108.3 all-reduce.9
  906.3 692.7 all-reduce.7
where the time goes:
time: 1640 us; the launch traced here: 1610 us
  waiting for transfers between devices  1460 us (89%)
  starting transfers between devices  42 us (3%)
  blocking collectives  41.4 us (3%)
  matrix products  34.9 us (2%)
    unnamed x7, waiting for transfers between devices  692 us
    all_gather x2, waiting for transfers between devices, per_device(): every_row = lax.all_gather(normed, 'yz', axis=0, tiled=True)  645 us
    reduce_scatter x2, waiting for transfers between devices, per_device(): lax.psum_scatter(jnp.dot(every_row, w_qkv, preferred_element_type=jnp.flo...  81.3 us
  transfers between devices with their start and end apart: 10, of which 9 were waited for; matrix products, arithmetic and copies ran while one was open for 2% of the time, Pallas kernels for 0%

commit v1 on v0

v1 whole, which is shorter than its diff:
```python
import functools

import jax
import jax.numpy as jnp
from jax import lax
from jax.experimental import pallas as pl
from jax.experimental.pallas import tpu as pltpu
from jax.sharding import PartitionSpec as P

D = 9216
HEADS = 24
HEAD_DIM = 256
CTX = 2048
STEPS = 2
EPS = 1e-06
SCALE = 0.0625
WIDTH = 2304
HALF = 1152
UNITS = 576
QCOLS = 104
OCOLS = 96
MESH = pl.DeviceIdType.MESH
F32 = jnp.float32
BF16 = jnp.bfloat16


class Place:
    def __init__(self):
        g = lax.axis_index("gx")
        j = lax.axis_index("yz")
        self.g, self.j = g, j
        self.zh, self.c = g // 2, g % 2
        self.x, self.z, self.y = j // 16, (j // 4) % 4, j % 4

    def along_x(self, d):
        t = (self.x + d) % 4
        return t, (self.g, t * 16 + self.z * 4 + self.y)

    def along_z(self, d):
        t = (self.z + d) % 4
        return t, (self.g, self.x * 16 + t * 4 + self.y)

    def along_y(self, d):
        t = (self.y + d) % 4
        return t, (self.g, self.x * 16 + self.z * 4 + t)

    def other_core(self):
        return (self.zh * 2 + (1 - self.c), self.j)

    def other_half(self):
        return ((1 - self.zh) * 2 + self.c, self.j)

    def gx_partner(self, d):
        return ((self.g + d) % 4, self.j)


def greet(me):
    barrier = pltpu.get_barrier_semaphore()
    for d in (1, 2, 3):
        for target in (me.along_x(d)[1], me.along_z(d)[1], me.along_y(d)[1], me.gx_partner(d)):
            pl.semaphore_signal(barrier, inc=1, device_id=target, device_id_type=MESH)
    pl.semaphore_wait(barrier, 12)


class Wire:
    def __init__(self, send_sems, recv_sems):
        self.send_sems, self.recv_sems = send_sems, recv_sems
        self.used = 0
        self.open = []

    def send(self, src, dst, target):
        copy = pltpu.make_async_remote_copy(
            src_ref=src,
            dst_ref=dst,
            send_sem=self.send_sems.at[self.used],
            recv_sem=self.recv_sems.at[self.used],
            device_id=target,
            device_id_type=MESH,
        )
        self.used += 1
        copy.start()
        self.open.append(copy)
        return copy

    def close(self):
        for copy in self.open:
            copy.wait_send()


def arrive(copies):
    for copy in copies:
        copy.wait_recv()


def dot(a, b):
    return jnp.dot(a, b, preferred_element_type=F32)


def dot_t(a, b):
    return lax.dot_general(a, b, (((1,), (1,)), ((), ())), preferred_element_type=F32)


def normalise(me, wire, hidden_ref, gain_ref, stats, shard):
    rows = jnp.concatenate([hidden_ref[0].astype(F32), hidden_ref[1].astype(F32)], 0)
    stats[3, 0] = jnp.broadcast_to(jnp.sum(rows, 1, keepdims=True), (8, 128))
    stats[3, 1] = jnp.broadcast_to(jnp.sum(rows * rows, 1, keepdims=True), (8, 128))
    arrive([wire.send(stats.at[3], stats.at[d - 1], me.gx_partner(d)) for d in (1, 2, 3)])
    total = (stats[0] + stats[1]) + (stats[2] + stats[3])
    mean = total[0, :, :1] / D
    var = total[1, :, :1] / D - mean * mean
    normed = (rows - mean) * lax.rsqrt(var + EPS) * gain_ref[...]
    shard[...] = jnp.concatenate([normed[:, :HALF], normed[:, HALF:]], 0).astype(BF16)


def gather_rows(me, wire, every):
    own = every.at[me.x, me.z, me.y]
    arrive([wire.send(own, own, me.along_z(d)[1]) for d in (1, 2, 3)])
    low = every.at[me.x, pl.ds(0, 2), me.y]
    high = every.at[me.x, pl.ds(2, 2), me.y]
    copies = []
    for d in (1, 2, 3):
        copies.append(wire.send(low, low, me.along_x(d)[1]))
        copies.append(wire.send(high, high, me.along_y(d)[1]))
    arrive(copies)
    low = every.at[:, pl.ds(0, 2), me.y]
    high = every.at[me.x, pl.ds(2, 2)]
    copies = []
    for d in (1, 2, 3):
        copies.append(wire.send(low, low, me.along_y(d)[1]))
        copies.append(wire.send(high, high, me.along_x(d)[1]))
    arrive(copies)


def unfold(every, normed):
    def body(i, _):
        block = every[i // 4, i % 4].astype(F32)
        rows = pl.ds(pl.multiple_of(i * 32, 32), 32)
        normed[rows, :HALF] = block[:, :8].reshape(32, HALF).astype(BF16)
        normed[rows, HALF:] = block[:, 8:].reshape(32, HALF).astype(BF16)
        return 0

    lax.fori_loop(0, 16, body, 0)


def first_products(me, m, normed, wq, wg, wu, qkv, gu):
    rows = normed[pl.ds(pl.multiple_of(m * 256, 256), 256), :]
    part = dot_t(rows, wq[...]).astype(BF16)
    gate = dot_t(rows, wg[...])
    up = dot_t(rows, wu[...])
    tail = jnp.concatenate([gate[:, 512:], up[:, 512:]], 1)
    for c in (0, 1):
        own = slice(128 * c, 128 * c + 128)
        qkv[m, c] = jnp.concatenate([part[own], jnp.zeros((128, 24), BF16)], 1)
        gu[m, c, :, :512] = gate[own, :512].astype(BF16)
        gu[m, c, :, 512:1024] = up[own, :512].astype(BF16)
        gu[m, c, :, 1024:] = tail[own].astype(BF16)


def add_into(out, a, b, rows=32):
    def body(i, _):
        at = pl.ds(pl.multiple_of(i * rows, rows), rows)
        out[at, :] = (a[at, :].astype(F32) + b[at, :].astype(F32)).astype(BF16)
        return 0

    lax.fori_loop(0, 128 // rows, body, 0)


def reduce_width(me, wire, normed, wq, wg, wu, qkv, gu, qkv_in, gu_in, qkv_far, gu_far):
    far = 1 - me.zh
    for m in (far, me.zh):
        first_products(me, m, normed, wq, wg, wu, qkv, gu)
        near = [
            wire.send(qkv.at[m, 1 - me.c], qkv_in.at[m], me.other_core()),
            wire.send(gu.at[m, 1 - me.c], gu_in.at[m], me.other_core()),
        ]
        arrive(near)
        add_into(qkv.at[m, me.c], qkv.at[m, me.c], qkv_in.at[m])
        if m is far:
            qkv_copy = wire.send(qkv.at[m, me.c], qkv_far, me.other_half())
        add_into(gu.at[m, me.c], gu.at[m, me.c], gu_in.at[m])
        if m is far:
            gu_copy = wire.send(gu.at[m, me.c], gu_far, me.other_half())
    return qkv_copy, gu_copy


def spread_qkv(me, wire, share, r1, q2, r2, r3):
    copies = []
    for d in (1, 2, 3):
        t, target = me.along_x(d)
        copies.append(wire.send(share.at[t], r1.at[me.x], target))
    r1[me.x] = share[me.x]
    arrive(copies)
    mixed = r1[...].astype(F32).reshape(4, 4, 8, 128)
    for t in range(4):
        q2[t] = mixed[:, t].reshape(32, 128).astype(BF16)
    copies = []
    for d in (1, 2, 3):
        t, target = me.along_z(d)
        copies.append(wire.send(q2.at[t], r2.at[me.z], target))
    r2[me.z] = q2[me.z]
    arrive(copies)
    copies = [wire.send(r2, r3.at[me.y], me.along_y(d)[1]) for d in (1, 2, 3)]
    r3[me.y] = r2[...]
    arrive(copies)
    row = lax.broadcasted_iota(jnp.int32, (128, 512), 0)
    col = lax.broadcasted_iota(jnp.int32, (128, 512), 1)
    wanted = (
        ((col >> 3) & 3) * 32
        + ((col >> 5) & 3) * 8
        + ((col >> 7) & 3) * 2
        + ((col >> 2) & 1)
    )
    pick = jnp.where((row == wanted) & ((col & 3) == me.y), 1.0, 0.0).astype(BF16)
    return dot(pick, r3[...].reshape(512, 128))


def collect_heads(me, wire, t_ref, r1, q2, r2, r3):
    copies = []
    for d in (1, 2, 3):
        t, target = me.along_x(d)
        copies.append(wire.send(t_ref.at[t], r1.at[me.x], target))
    r1[me.x] = t_ref[me.x]
    arrive(copies)
    mixed = r1[...].astype(F32).reshape(4, 4, 8, 128)
    for t in range(4):
        q2[t] = mixed[:, t].reshape(32, 128).astype(BF16)
    copies = []
    for d in (1, 2, 3):
        t, target = me.along_z(d)
        copies.append(wire.send(q2.at[t], r2.at[me.z], target))
    r2[me.z] = q2[me.z]
    arrive(copies)
    copies = [wire.send(r2, r3.at[me.y], me.along_y(d)[1]) for d in (1, 2, 3)]
    r3[me.y] = r2[...]
    arrive(copies)
    row = lax.broadcasted_iota(jnp.int32, (128, 512), 0)
    col = lax.broadcasted_iota(jnp.int32, (128, 512), 1)
    wanted = (
        ((col >> 3) & 3) * 32
        + ((col >> 5) & 3) * 8
        + (col & 1) * 4
        + ((col >> 7) & 3)
    )
    pick = jnp.where((row == wanted) & (((col >> 1) & 3) == me.y), 1.0, 0.0).astype(BF16)
    return dot(pick, r3[...].reshape(512, 128)).astype(BF16)


def share_blocks(me, wire, blocks):
    own = blocks.at[me.zh, me.c]
    arrive([wire.send(own, own, me.other_half())])
    pair = blocks.at[:, me.c]
    arrive([wire.send(pair, pair, me.other_core())])


def activate(gu, gu_far, out):
    def body(i, _):
        at = pl.ds(pl.multiple_of(i * 32, 32), 32)
        total = gu[at, :].astype(F32) + gu_far[at, :].astype(F32)
        gate, up = total[:, :512], total[:, 512:1024]
        out[at, :512] = (gate / (1.0 + jnp.exp(-gate)) * up).astype(BF16)
        tail = total[:, 1024:]
        last = tail / (1.0 + jnp.exp(-tail)) * pltpu.roll(tail, 64, 1)
        lane = lax.broadcasted_iota(jnp.int32, last.shape, 1)
        out[at, 512:] = jnp.where(lane < 64, last, 0.0).astype(BF16)
        return 0

    lax.fori_loop(0, 4, body, 0)


def kernel_one(
    hidden_ref, gain_ref, wq, wg, wu, qkv_out, hidden_out,
    stats, every, normed, qkv, gu, qkv_in, gu_in, qkv_far, gu_far, share, r1, q2, r2, r3, blocks,
    send_sems, recv_sems,
):
    me = Place()
    wire = Wire(send_sems, recv_sems)
    greet(me)
    normalise(me, wire, hidden_ref, gain_ref, stats, every.at[me.x, me.z, me.y])
    gather_rows(me, wire, every)
    unfold(every, normed)
    qkv_copy, gu_copy = reduce_width(
        me, wire, normed, wq, wg, wu, qkv, gu, qkv_in, gu_in, qkv_far, gu_far
    )
    arrive([qkv_copy])
    whole = qkv[me.zh, me.c].astype(F32) + qkv_far[...].astype(F32)
    share[...] = whole.astype(BF16).reshape(4, 32, 128)
    qkv_out[...] = spread_qkv(me, wire, share, r1, q2, r2, r3)
    arrive([gu_copy])
    activate(gu.at[me.zh, me.c], gu_far, blocks.at[me.zh, me.c])
    share_blocks(me, wire, blocks)
    hidden_out[...] = blocks[...]
    wire.close()


def kernel_attend(lengths_ref, qkv_ref, cache_ref, out_ref, flat, heads, fresh_k, fresh_v, flat_out):
    for j in range(64):
        flat[:, QCOLS * j : QCOLS * j + QCOLS] = qkv_ref[2 * j : 2 * j + 2, :QCOLS]
    for h in range(HEADS + 1):
        heads[2 * h : 2 * h + 2, :] = flat[:, 256 * h : 256 * h + 256]
    length = lengths_ref[0]
    count = 2 * HEADS + 8
    row = lax.broadcasted_iota(jnp.int32, (count, 1), 0)
    lane = lax.broadcasted_iota(jnp.int32, (8, 128), 1).astype(F32)
    freqs = 10000.0 ** (-lane / 128.0)
    step8 = (lax.broadcasted_iota(jnp.int32, (8, 128), 0) & 1).astype(F32)
    angle = (length.astype(F32) + step8) * freqs
    cosine = jnp.cos(angle)
    sine = jnp.sin(angle)
    cosine = jnp.concatenate([cosine] * (count // 8), 0)
    sine = jnp.concatenate([sine] * (count // 8), 0)
    first, second = heads[:count, :128], heads[:count, 128:]
    turned = jnp.concatenate(
        [first * cosine - second * sine, second * cosine + first * sine], 1
    )
    queries = turned[: 2 * HEADS].astype(BF16)
    in_use = lax.broadcasted_iota(jnp.int32, (16, 256), 0) < 2
    fresh_k[...] = jnp.where(
        in_use, jnp.concatenate([turned[2 * HEADS :], turned[2 * HEADS :]], 0), 0.0
    ).astype(BF16)
    fresh_v[...] = jnp.zeros((16, 256), F32)
    fresh_v[0:2, :] = flat[:, 6400:6656]
    keys = cache_ref[0, :, :256]
    values = cache_ref[0, :, 256:]
    old = dot_t(queries, keys) * SCALE
    slot = lax.broadcasted_iota(jnp.int32, old.shape, 1)
    old = jnp.where(slot < length, old, -1e30)
    new = dot_t(queries, fresh_k[...]) * SCALE
    new_slot = lax.broadcasted_iota(jnp.int32, new.shape, 1)
    new_step = lax.broadcasted_iota(jnp.int32, new.shape, 0) & 1
    new = jnp.where(new_slot <= new_step, new, -1e30)
    peak = jnp.maximum(jnp.max(old, 1, keepdims=True), jnp.max(new, 1, keepdims=True))
    old = jnp.exp(old - peak)
    new = jnp.exp(new - peak)
    total = jnp.sum(old, 1, keepdims=True) + jnp.sum(new, 1, keepdims=True)
    mixed = dot((old / total).astype(BF16), values) + dot(
        (new / total).astype(BF16), fresh_v[...].astype(BF16)
    )
    heads[: 2 * HEADS, :] = mixed
    for h in range(HEADS):
        flat_out[:, 256 * h : 256 * h + 256] = heads[2 * h : 2 * h + 2, :]
    out_ref[...] = jnp.zeros((128, 128), F32)
    for j in range(64):
        out_ref[2 * j : 2 * j + 2, :OCOLS] = flat_out[:, OCOLS * j : OCOLS * j + OCOLS]


def second_products(hidden, heads, wo, wd, partial):
    def body(m, _):
        lines = hidden[m].reshape(256, 640)
        attended = heads[m].reshape(256, 128)[:, :OCOLS]
        for n in range(0, HALF, 384):
            sides = []
            for at in (n, HALF + n):
                columns = slice(at, at + 384)
                product = (
                    dot(lines[:, :512], wd[:512, columns])
                    + dot(lines[:, 512:UNITS], wd[512:, columns])
                    + dot(attended, wo[:, columns])
                )
                sides.append(product.reshape(2, 4, 4, 8, 384))
            partial[pl.ds(m * 2, 2), :, :, :, n : n + 384] = jnp.concatenate(sides, 3).astype(BF16)
        return 0

    lax.fori_loop(0, 2, body, 0)


def scatter_rows(me, wire, partial, ra, rb, sa, sb, ra2, rb2, sz, rz):
    copies = []
    for d in (1, 2, 3):
        t, target = me.along_y(d)
        copies.append(wire.send(partial.at[:, pl.ds(0, 2), t], ra.at[d - 1], target))
        t, target = me.along_x(d)
        copies.append(wire.send(partial.at[t, pl.ds(2, 2)], rb.at[d - 1], target))
    arrive(copies)

    def add_low(i, _):
        total = partial[i, pl.ds(0, 2), me.y].astype(F32)
        for d in range(3):
            total = total + ra[d, i].astype(F32)
        sa[i] = total.astype(BF16)
        return 0

    lax.fori_loop(0, 4, add_low, 0)

    def add_high(i, _):
        total = partial[me.x, 2 + i // 2, pl.ds((i % 2) * 2, 2)].astype(F32)
        for d in range(3):
            total = total + rb[d, i // 2, pl.ds((i % 2) * 2, 2)].astype(F32)
        sb[i // 2, pl.ds((i % 2) * 2, 2)] = total.astype(BF16)
        return 0

    lax.fori_loop(0, 4, add_high, 0)
    copies = []
    for d in (1, 2, 3):
        t, target = me.along_x(d)
        copies.append(wire.send(sa.at[t], ra2.at[d - 1], target))
        t, target = me.along_y(d)
        copies.append(wire.send(sb.at[:, t], rb2.at[d - 1], target))
    arrive(copies)
    low = sa[me.x].astype(F32)
    high = sb[:, me.y].astype(F32)
    for d in range(3):
        low = low + ra2[d].astype(F32)
        high = high + rb2[d].astype(F32)
    sz[0:2] = low.astype(BF16)
    sz[2:4] = high.astype(BF16)
    copies = []
    for d in (1, 2, 3):
        t, target = me.along_z(d)
        copies.append(wire.send(sz.at[t], rz.at[d - 1], target))
    arrive(copies)
    total = sz[me.z].astype(F32)
    for d in range(3):
        total = total + rz[d].astype(F32)
    return total


def finish(hidden_ref, total, out_ref):
    whole = jnp.concatenate([total[:8], total[8:]], 1)
    for step in range(STEPS):
        rows = whole[4 * step : 4 * step + 4]
        out_ref[step] = (hidden_ref[step].astype(F32) + rows).astype(BF16)


def kernel_two(
    hidden_ref, heads_ref, lines, wo, wd, out_ref,
    t_ref, r1, q2, r2, r3, heads, partial, ra, rb, sa, sb, ra2, rb2, sz, rz,
    send_sems, recv_sems,
):
    me = Place()
    wire = Wire(send_sems, recv_sems)
    greet(me)
    t_ref[...] = heads_ref[...].astype(BF16).reshape(4, 32, 128)
    heads[me.zh, me.c] = collect_heads(me, wire, t_ref, r1, q2, r2, r3)
    share_blocks(me, wire, heads)
    second_products(lines, heads, wo, wd, partial)
    total = scatter_rows(me, wire, partial, ra, rb, sa, sb, ra2, rb2, sz, rz)
    finish(hidden_ref, total, out_ref)
    wire.close()


VM = pl.BlockSpec(memory_space=pltpu.VMEM)
A2A_SCRATCH = [
    pltpu.VMEM((4, 32, 128), BF16),
    pltpu.VMEM((4, 32, 128), BF16),
    pltpu.VMEM((4, 32, 128), BF16),
    pltpu.VMEM((4, 32, 128), BF16),
    pltpu.VMEM((4, 4, 32, 128), BF16),
]


def per_device(hidden_in, norm_gain, w_qkv, w_gate, w_up, w_out, w_down, kv_cache, lengths):
    qkv, hidden = pl.pallas_call(
        kernel_one,
        name="first_half",
        out_shape=(
            jax.ShapeDtypeStruct((128, 128), F32),
            jax.ShapeDtypeStruct((2, 2, 128, 640), BF16),
        ),
        in_specs=[VM] * 5,
        out_specs=(VM, VM),
        scratch_shapes=[
            pltpu.VMEM((4, 2, 8, 128), F32),
            pltpu.VMEM((4, 4, 4, 16, HALF), BF16),
            pltpu.VMEM((512, WIDTH), BF16),
            pltpu.VMEM((2, 2, 128, 128), BF16),
            pltpu.VMEM((2, 2, 128, 2 * UNITS), BF16),
            pltpu.VMEM((2, 128, 128), BF16),
            pltpu.VMEM((2, 128, 2 * UNITS), BF16),
            pltpu.VMEM((128, 128), BF16),
            pltpu.VMEM((128, 2 * UNITS), BF16),
        ]
        + A2A_SCRATCH
        + [
            pltpu.VMEM((2, 2, 128, 640), BF16),
            pltpu.SemaphoreType.DMA((40,)),
            pltpu.SemaphoreType.DMA((40,)),
        ],
        compiler_params=pltpu.CompilerParams(
            collective_id=0, has_side_effects=True, vmem_limit_bytes=48 * 2**20
        ),
    )(hidden_in, norm_gain.reshape(1, WIDTH), w_qkv.T, w_gate.T, w_up.T)
    heads = pl.pallas_call(
        kernel_attend,
        name="attend",
        out_shape=jax.ShapeDtypeStruct((128, 128), F32),
        in_specs=[pl.BlockSpec(memory_space=pltpu.SMEM), VM, VM],
        out_specs=VM,
        scratch_shapes=[
            pltpu.VMEM((2, 6656), F32),
            pltpu.VMEM((56, 256), F32),
            pltpu.VMEM((16, 256), BF16),
            pltpu.VMEM((16, 256), F32),
            pltpu.VMEM((2, 6144), F32),
        ],
        compiler_params=pltpu.CompilerParams(vmem_limit_bytes=32 * 2**20),
    )(lengths, qkv, kv_cache)
    return pl.pallas_call(
        kernel_two,
        name="second_half",
        out_shape=jax.ShapeDtypeStruct((2, 4, WIDTH), BF16),
        in_specs=[VM] * 5,
        out_specs=VM,
        scratch_shapes=A2A_SCRATCH
        + [
            pltpu.VMEM((2, 2, 128, 128), BF16),
            pltpu.VMEM((4, 4, 4, 16, HALF), BF16),
            pltpu.VMEM((3, 4, 2, 16, HALF), BF16),
            pltpu.VMEM((3, 2, 4, 16, HALF), BF16),
            pltpu.VMEM((4, 2, 16, HALF), BF16),
            pltpu.VMEM((2, 4, 16, HALF), BF16),
            pltpu.VMEM((3, 2, 16, HALF), BF16),
            pltpu.VMEM((3, 2, 16, HALF), BF16),
            pltpu.VMEM((4, 16, HALF), BF16),
            pltpu.VMEM((3, 16, HALF), BF16),
            pltpu.SemaphoreType.DMA((40,)),
            pltpu.SemaphoreType.DMA((40,)),
        ],
        compiler_params=pltpu.CompilerParams(
            collective_id=1, has_side_effects=True, vmem_limit_bytes=48 * 2**20
        ),
    )(hidden_in, heads, hidden, w_out, w_down)


def solution(mesh):
    return jax.shard_map(
        per_device,
        mesh=mesh,
        in_specs=(
            P(None, "yz", "gx"),
            P("gx"),
            P("gx", "yz"),
            P("gx", "yz"),
            P("gx", "yz"),
            P("yz", "gx"),
            P("yz", "gx"),
            P(("gx", "yz"), None, None),
            P(("gx", "yz")),
        ),
        out_specs=P(None, "yz", "gx"),
        check_vma=False,
    )
```

time: 1640 us -> 135 us (0.08); the launches traced: 1610 us -> 134 us
  waiting for transfers between devices: 1460 us -> 0 us
  Pallas kernels: 0 us -> 128 us
  starting transfers between devices: 42 us -> 0 us
  blocking collectives: 41.4 us -> 0 us
  matrix products: 34.9 us -> 0 us
    unnamed x7 -> x0, waiting for transfers between devices: 692 us -> none
    all_gather x2 -> x0, waiting for transfers between devices: 645 us -> none  [per_device(): every_row = lax.all_gather(normed, 'yz', axis=0, tiled=True)]
    pallas_call x0 -> x3, Pallas kernels: none -> 128 us  [the longest x1 76.8 us: per_device(): pl.pallas_call(kernel_one, name='first_half', out_shape=(jax.ShapeDtypeSt...]
    reduce_scatter x2 -> x0, waiting for transfers between devices: 81.3 us -> none  [per_device(): lax.psum_scatter(jnp.dot(every_row, w_qkv, preferred_element_type=jnp.flo...]
    all_to_all x4 -> x0, starting transfers between devices: 41.7 us -> none  [the longest x2 25.3 us: per_device(): lax.all_to_all(attended, 'yz', split_axis=1, concat_axis=0, tiled=True)]
    dot_general x17 -> x0, matrix products: 34.9 us -> none  [the longest x2 7.86 us: per_device(): jnp.dot(every_row, w_gate, preferred_element_type=jnp.float32)]
    all_gather x2 -> x0, blocking collectives: 24.9 us -> none  [per_device(): head_rows = lax.all_gather(head_block, 'gx', axis=0, tiled=True)]
    all_to_all x4 -> x0, waiting for transfers between devices: 23 us -> none  [the longest x2 13.9 us: per_device(): lax.all_to_all(attended, 'yz', split_axis=1, concat_axis=0, tiled=True)]
  transfers between devices with their start and end apart: 10 -> 0, of which waited for: 9 -> 0; matrix products, arithmetic and copies ran while one was open for 2% -> 0% of each run, Pallas kernels for 0% -> 0%
where the time goes in v1:
time: 135 us; the launch traced here: 134 us
  Pallas kernels  128 us (95%)
  local copies, waits for them, and re-layouts  4.88 us (4%)
    pallas_call x1, Pallas kernels, per_device(): pl.pallas_call(kernel_one, name='first_half', out_shape=(jax.ShapeDtypeSt...  76.8 us
    pallas_call x1, Pallas kernels, per_device(): pl.pallas_call(kernel_two, name='second_half', out_shape=jax.ShapeDtypeSt...  50.2 us
    unnamed x13, local copies, waits for them, and re-layouts  4.17 us

profile of v1, /device:TPU:2, one launch (start us, length us, event | category | flops | bytes accessed | tf_op | source)
XLA Modules:
  0.0 133.9 jit_solution(8440407726983036164)
XLA Ops:
  0.7 0.7 reshape.3.gain_ref
  1.4 0.0 copy-start
  1.4 1.7 %copy-done = bf16[2304,576]{0,1:T(8,128)(2,1)S(1)} copy-done((bf16[2304,576]{0,1:T(8,128)(2,1)S(1)}, bf16[2304,576]{0,1:T(8,128)(2,1)}, u32[]{:S(2)}) %copy-start) | copy-done | bytes 2654232
  3.1 0.0 copy-start.3
  3.1 1.0 copy-done.3
  4.1 0.0 copy-start.5
  4.1 0.8 copy-done.5
  4.9 0.0 copy-start.2
  4.9 0.0 copy-start.1
  4.9 0.0 copy-start.4
  4.9 76.8 %first_half.1 = (f32[128,128]{1,0:T(8,128)S(1)}, bf16[2,2,128,640]{3,2,1,0:T(8,128)(2,1)S(1)}) custom-call(bf16[2,4,2304]{2,1,0:T(4,128)(2,1)S(1)} %copy-done.5, f32[1,2304]{1,0:T(1,128)S(1)} %reshape.3.gain_ref, bf16[104,2304]{1,0:T(8,128)(2,1)S(1)} %bitcast.4, bf16[576,2304]{1,0:T(8,128)(2,1)S(1)} %bitcast.3, bf16[576,2304]{1,0:T(8,128)(2,1)} %bitcast.5), custom_call_target="tpu_custom_call" | custom-call | tf_op jit(solution)/shard_map/first_half/pallas_call | solution.py:452
  81.7 0.0 copy-done.2
  81.7 1.4 %attend.1.heads_ref = f32[128,128]{1,0:T(8,128)S(1)} custom-call(s32[1]{0:T(128)S(6)} %copy.11.lengths_ref, f32[128,128]{1,0:T(8,128)S(1)} %get-tuple-element.7.qkv_ref, bf16[1,2048,512]{2,1,0:T(8,128)(2,1)S(1)} %copy-done.2), custom_call_target="tpu_custom_call" | custom-call | tf_op jit(solution)/shard_map/attend/pallas_call | solution.py:482
  83.1 0.0 copy-done.1
  83.1 0.0 copy-done.4
  83.1 50.2 %second_half.1 = bf16[2,4,2304]{2,1,0:T(4,128)(2,1)S(1)} custom-call(bf16[2,4,2304]{2,1,0:T(4,128)(2,1)S(1)} %copy-done.5, f32[128,128]{1,0:T(8,128)S(1)} %attend.1.heads_ref, bf16[2,2,128,640]{3,2,1,0:T(8,128)(2,1)S(1)} %get-tuple-element.8.lines, bf16[96,2304]{1,0:T(8,128)(2,1)S(1)} %copy-done.4, bf16[576,2304]{1,0:T(8,128)(2,1)S(1)} %copy-done.1), custom_call_target="tpu_custom_call" | custom-call | tf_op jit(solution)/shard_map/second_half/pallas_call | solution.py:497
  133.3 0.6 copy.12
Async XLA Ops:
  1.4 1.7 %copy-start = (bf16[2304,576]{0,1:T(8,128)(2,1)S(1)}, bf16[2304,576]{0,1:T(8,128)(2,1)}, u32[]{:S(2)}) copy-start(bf16[2304,576]{0,1:T(8,128)(2,1)} %param.12) | copy-start | bytes 7962628
  3.1 1.0 copy-start.3
  4.1 0.8 copy-start.5
  4.9 76.8 %copy-start.2 = (bf16[1,2048,512]{2,1,0:T(8,128)(2,1)S(1)}, bf16[1,2048,512]{2,1,0:T(8,128)(2,1)}, u32[]{:S(2)}) copy-start(bf16[1,2048,512]{2,1,0:T(8,128)(2,1)} %cache_ref.1) | copy-start | bytes 6291460
  4.9 78.2 %copy-start.1 = (bf16[576,2304]{1,0:T(8,128)(2,1)S(1)}, bf16[576,2304]{1,0:T(8,128)(2,1)}, u32[]{:S(2)}) copy-start(bf16[576,2304]{1,0:T(8,128)(2,1)} %wd.1) | copy-start | bytes 7962628
  4.9 78.2 %copy-start.4 = (bf16[96,2304]{1,0:T(8,128)(2,1)S(1)}, bf16[96,2304]{1,0:T(8,128)(2,1)}, u32[]{:S(2)}) copy-start(bf16[96,2304]{1,0:T(8,128)(2,1)} %wo.1) | copy-start | bytes 1327108

commit v2 on v0

v2 whole, which is shorter than its diff:
```python
import jax
import jax.numpy as jnp
from jax import lax
from jax.experimental import pallas as pl
from jax.experimental.pallas import tpu as pltpu
from jax.sharding import PartitionSpec as P

D = 9216
HEADS = 24
HEAD_DIM = 256
CTX = 2048
STEPS = 2
EPS = 1e-06
SCALE = 0.0625
WIDTH = 2304
HALF = 1152
UNITS = 576
QCOLS = 104
OCOLS = 96
MESH = pl.DeviceIdType.MESH
F32 = jnp.float32
BF16 = jnp.bfloat16


class Place:
    def __init__(self):
        g = lax.axis_index("gx")
        j = lax.axis_index("yz")
        self.g, self.j = g, j
        self.zh, self.c = g // 2, g % 2
        self.x, self.z, self.y = j // 16, (j // 4) % 4, j % 4

    def at(self, zh=0, c=0, x=0, z=0, y=0):
        g = ((self.zh + zh) % 2) * 2 + (self.c + c) % 2
        j = ((self.x + x) % 4) * 16 + ((self.z + z) % 4) * 4 + (self.y + y) % 4
        return (g, j)


def greet(me):
    barrier = pltpu.get_barrier_semaphore()
    count = 0
    for d in (1, 2, 3):
        partners = [me.at(x=d), me.at(z=d), me.at(y=d), me.at(c=1, x=d), me.at(zh=1, z=d)]
        partners.append(me.at(zh=d // 2, c=d % 2))
        for target in partners:
            pl.semaphore_signal(barrier, inc=1, device_id=target, device_id_type=MESH)
            count += 1
    pl.semaphore_wait(barrier, count)


class Wire:
    def __init__(self, send_sems, recv_sems):
        self.send_sems, self.recv_sems = send_sems, recv_sems
        self.used = 0
        self.open = []

    def send(self, src, dst, target):
        copy = pltpu.make_async_remote_copy(
            src_ref=src,
            dst_ref=dst,
            send_sem=self.send_sems.at[self.used],
            recv_sem=self.recv_sems.at[self.used],
            device_id=target,
            device_id_type=MESH,
        )
        self.used += 1
        copy.start()
        self.open.append(copy)
        return copy

    def close(self):
        for copy in self.open:
            copy.wait_send()


def arrive(copies):
    for copy in copies:
        copy.wait_recv()


def dot(a, b):
    return jnp.dot(a, b, preferred_element_type=F32)


def dot_t(a, b):
    return lax.dot_general(a, b, (((1,), (1,)), ((), ())), preferred_element_type=F32)


def fold(hidden, own, stats):
    rows = jnp.concatenate([hidden[0].astype(F32), hidden[1].astype(F32)], 0)
    own[...] = jnp.concatenate([rows[:, :HALF], rows[:, HALF:]], 0).astype(BF16)
    stats[0, 0] = jnp.broadcast_to(jnp.sum(rows, 1, keepdims=True), (8, 128))
    stats[0, 1] = jnp.broadcast_to(jnp.sum(rows * rows, 1, keepdims=True), (8, 128))


def moments(stats):
    total = (stats[0] + stats[1]) + (stats[2] + stats[3])
    mean = total[0] / D
    var = total[1] / D - mean * mean
    lane = lax.broadcasted_iota(jnp.int32, (8, 128), 1)
    return jnp.where(lane < 64, mean, lax.rsqrt(var + EPS))


def normalise(me, p, every, known, gain, normed):
    def body(i, _):
        z = (me.z + 2 * p + i // 4) % 4
        block = every[z, i % 4].astype(F32)
        about = known[i % 4, z].reshape(32, 128)
        mean, scale = about[:, :1], about[:, 64:65]
        left = (block[:, :8].reshape(32, HALF) - mean) * scale * gain[:, :HALF]
        right = (block[:, 8:].reshape(32, HALF) - mean) * scale * gain[:, HALF:]
        rows = pl.ds(pl.multiple_of(p * 256 + i * 32, 32), 32)
        normed[rows, :HALF] = left.astype(BF16)
        normed[rows, HALF:] = right.astype(BF16)
        return 0

    lax.fori_loop(0, 8, body, 0)


def qkv_products(p, normed, wq, qkv):
    part = dot_t(normed[256 * p : 256 * p + 256, :], wq[...])
    part = jnp.concatenate([part, jnp.zeros((256, 24), F32)], 1)
    qkv[2 * p : 2 * p + 2] = part.reshape(2, 2, 2, 32, 128).astype(BF16)


def gate_up_products(p, normed, wg, wu, gu):
    rows = normed[256 * p : 256 * p + 256, :]
    gate = dot_t(rows, wg[...])
    up = dot_t(rows, wu[...])
    tail = jnp.concatenate([gate[:, 512:], up[:, 512:]], 1)
    own = slice(2 * p, 2 * p + 2)
    gu[own, :, :, :, :512] = gate[:, :512].reshape(2, 2, 2, 32, 512).astype(BF16)
    gu[own, :, :, :, 512:1024] = up[:, :512].reshape(2, 2, 2, 32, 512).astype(BF16)
    gu[own, :, :, :, 1024:] = tail.reshape(2, 2, 2, 32, 128).astype(BF16)


def add_cores(me, p, half, gu, gu_in, gu_sum):
    def body(e, _):
        total = gu[2 * p + e, half, me.c].astype(F32) + gu_in[p, e, half].astype(F32)
        gu_sum[p, half, e] = total.astype(BF16)
        return 0

    lax.fori_loop(0, 2, body, 0)


def activate(me, p, gu_sum, gu_far, blocks):
    def body(e, _):
        total = gu_sum[p, me.zh, e].astype(F32) + gu_far[p, e].astype(F32)
        gate, up = total[:, :512], total[:, 512:1024]
        tail = total[:, 1024:]
        last = tail / (1.0 + jnp.exp(-tail)) * pltpu.roll(tail, 64, 1)
        lane = lax.broadcasted_iota(jnp.int32, last.shape, 1)
        blocks[2 * p + e, me.zh, me.c, :, :512] = (gate / (1.0 + jnp.exp(-gate)) * up).astype(BF16)
        blocks[2 * p + e, me.zh, me.c, :, 512:] = jnp.where(lane < 64, last, 0.0).astype(BF16)
        return 0

    lax.fori_loop(0, 2, body, 0)


def two_way(me, wire, along, other, piece, landing):
    copies = []
    for b in (0, 1):
        for d in range(4):
            if b or d:
                target = me.at(**{other: b, along: d})
                copies.append(wire.send(piece(b, d), landing.at[b, getattr(me, along)], target))
    return copies


def attend(length, g_ref, cache, t_ref, flat, heads, fresh_v, flat_out, t_wide):
    for j in range(64):
        flat[:, QCOLS * j : QCOLS * j + QCOLS] = g_ref[2 * j : 2 * j + 2, :QCOLS]
    heads[48:56, :] = jnp.zeros((8, 256), F32)
    for h in range(HEADS + 1):
        heads[2 * h : 2 * h + 2, :] = flat[:, 256 * h : 256 * h + 256]
    lane = lax.broadcasted_iota(jnp.int32, (8, 128), 1).astype(F32)
    freqs = 10000.0 ** (-lane / 128.0)
    step8 = (lax.broadcasted_iota(jnp.int32, (8, 128), 0) & 1).astype(F32)
    angle = (length.astype(F32) + step8) * freqs
    cosine = jnp.concatenate([jnp.cos(angle)] * 7, 0)
    sine = jnp.concatenate([jnp.sin(angle)] * 7, 0)
    first, second = heads[:, :128], heads[:, 128:]
    turned = jnp.concatenate(
        [first * cosine - second * sine, second * cosine + first * sine], 1
    )
    queries = turned[: 2 * HEADS].astype(BF16)
    fresh = turned[2 * HEADS :]
    fresh_k = jnp.concatenate([fresh, jnp.zeros((8, 256), F32)], 0).astype(BF16)
    fresh_v[...] = jnp.zeros((16, 256), F32)
    fresh_v[0:2, :] = flat[:, 6400:6656]
    keys = cache[0, :, :256]
    values = cache[0, :, 256:]
    old = dot_t(queries, keys) * SCALE
    slot = lax.broadcasted_iota(jnp.int32, old.shape, 1)
    old = jnp.where(slot < length, old, -1e30)
    new = dot_t(queries, fresh_k) * SCALE
    new_slot = lax.broadcasted_iota(jnp.int32, new.shape, 1)
    new_step = lax.broadcasted_iota(jnp.int32, new.shape, 0) & 1
    new = jnp.where(new_slot <= new_step, new, -1e30)
    peak = jnp.maximum(jnp.max(old, 1, keepdims=True), jnp.max(new, 1, keepdims=True))
    old = jnp.exp(old - peak)
    new = jnp.exp(new - peak)
    total = jnp.sum(old, 1, keepdims=True) + jnp.sum(new, 1, keepdims=True)
    mixed = dot((old / total).astype(BF16), values) + dot(
        (new / total).astype(BF16), fresh_v[...].astype(BF16)
    )
    heads[: 2 * HEADS, :] = mixed
    for h in range(HEADS):
        flat_out[:, 256 * h : 256 * h + 256] = heads[2 * h : 2 * h + 2, :]
    t_wide[...] = jnp.zeros((128, 128), F32)
    for j in range(64):
        t_wide[2 * j : 2 * j + 2, :OCOLS] = flat_out[:, OCOLS * j : OCOLS * j + OCOLS]
    t_ref[...] = t_wide[...].astype(BF16).reshape(4, 32, 128)


def write_picks(me, pick_in, pick_mid, pick_out):
    def write(pick, wanted, keep):
        rows, depth = pick.shape
        row = lax.broadcasted_iota(jnp.int32, (64, depth), 0)
        col = lax.broadcasted_iota(jnp.int32, (64, depth), 1)
        place = jnp.where(keep(col), wanted(col), -1)

        def body(i, _):
            at = pl.ds(pl.multiple_of(i * 64, 64), 64)
            pick[at, :] = jnp.where(row + i * 64 == place, 1.0, 0.0).astype(BF16)
            return 0

        lax.fori_loop(0, rows // 64, body, 0)

    def bits(k, low, count):
        return (k >> low) & ((1 << count) - 1)

    def arrived(k):
        return bits(k, 3, 2) * 32 + bits(k, 5, 2) * 8 + bits(k, 7, 2) * 2 + bits(k, 2, 1)

    def sorted_by_y(k):
        return (
            bits(k, 1, 2) * 128 + bits(k, 8, 1) * 64 + bits(k, 5, 1) * 32
            + bits(k, 6, 2) * 8 + bits(k, 3, 2) * 2 + bits(k, 0, 1)
        )

    def by_row(k):
        chunk = (bits(k, 1, 2) - me.z) & 3
        block = ((bits(k, 6, 1) + me.zh) & 1) * 2 + ((bits(k, 5, 1) + me.c) & 1)
        return chunk * 128 + block * 32 + bits(k, 3, 2) * 8 + bits(k, 0, 1) * 4 + bits(k, 7, 2)

    write(pick_in, arrived, lambda k: bits(k, 0, 2) == me.y)
    write(pick_mid, sorted_by_y, lambda k: k >= 0)
    write(pick_out, by_row, lambda k: k >= 0)


def second_products(p, blocks, heads, wo, wd, partial):
    lines = blocks[2 * p : 2 * p + 2].reshape(256, 640)
    attended = heads[256 * p : 256 * p + 256, :OCOLS]
    for n in range(0, HALF, 384):
        sides = []
        for at in (n, HALF + n):
            columns = slice(at, at + 384)
            product = (
                dot(lines[:, :512], wd[:512, columns])
                + dot(lines[:, 512:UNITS], wd[512:, columns])
                + dot(attended, wo[:, columns])
            )
            sides.append(product.reshape(2, 4, 4, 8, 384))
        partial[2 * p : 2 * p + 2, :, :, :, n : n + 384] = jnp.concatenate(sides, 3).astype(BF16)


def kernel(
    lengths_ref, hidden_hbm, gain_hbm, wq_hbm, wg_hbm, wu_hbm, wo_hbm, wd_hbm, cache_hbm, out_ref,
    hidden, gain, wq, wg, wu, wo, wd, cache, load_sems,
    stats, known, every, normed, qkv, gu, gu_in, gu_sum, gu_far, blocks,
    s1, q2, s2, s2_sum, s3, g_ref, t_ref, flat, heads32, fresh_v, flat_out, t_wide,
    u1, u1_sorted, u2, u2_sorted, u3, heads, pick_in, pick_mid, pick_out,
    partial, ra, sa, rb, sz, rz,
    send_sems, recv_sems,
):
    me = Place()
    wire = Wire(send_sems, recv_sems)
    loads = []
    for i, (src, dst) in enumerate(
        (
            (hidden_hbm, hidden), (gain_hbm, gain), (wq_hbm, wq), (wg_hbm, wg),
            (wu_hbm, wu), (cache_hbm, cache), (wo_hbm, wo), (wd_hbm, wd),
        )
    ):
        loads.append(pltpu.make_async_copy(src, dst, load_sems.at[i]))
        loads[-1].start()
    loads[0].wait()
    fold(hidden, every.at[me.z, me.x, me.y], stats)
    greet(me)

    first_axis = ("x", "y", "x", "y")
    last_axis = ("y", "x", "y", "x")

    def send_own(e):
        z = (me.z + e) % 4
        own = every.at[z, me.x, me.y]
        return [wire.send(own, own, me.at(**{first_axis[e]: d})) for d in (1, 2, 3)]

    def send_line(e):
        z = (me.z + e) % 4
        line = every.at[z, :, me.y] if first_axis[e] == "x" else every.at[z, me.x]
        return [wire.send(line, line, me.at(**{last_axis[e]: d})) for d in (1, 2, 3)]

    own = every.at[me.z, me.x, me.y]
    sums = [wire.send(stats.at[0], stats.at[d], me.at(zh=d // 2, c=d % 2)) for d in (1, 2, 3)]
    shards = [wire.send(own, own, me.at(z=d)) for d in (1, 2, 3)]
    owns = [send_own(0)]
    arrive(shards)
    owns += [send_own(e) for e in (1, 2, 3)]
    arrive(owns[0])
    lines = [send_line(0)]
    arrive(sums)
    known[me.x, me.z, me.y] = moments(stats)
    mine = known.at[me.x, me.z, me.y]
    facts = [wire.send(mine, mine, me.at(z=d)) for d in (1, 2, 3)]
    for e in (1, 2, 3):
        arrive(owns[e])
        lines.append(send_line(e))
    arrive(facts)
    mine = known.at[me.x, :, me.y]
    facts = [wire.send(mine, mine, me.at(x=d)) for d in (1, 2, 3)]
    write_picks(me, pick_in, pick_mid, pick_out)
    arrive(facts)
    mine = known.at[:, :, me.y]
    facts = [wire.send(mine, mine, me.at(y=d)) for d in (1, 2, 3)]
    for i in (1, 2, 3, 4):
        loads[i].wait()
    arrive(facts)

    far = 1 - me.zh
    near, across = [None, None], [None, None]

    def send_core(p):
        src = gu.at[pl.ds(2 * p, 2), :, 1 - me.c]
        near[p] = wire.send(src, gu_in.at[p], me.at(c=1))

    def send_far(p):
        arrive([near[p]])
        add_cores(me, p, far, gu, gu_in, gu_sum)
        across[p] = wire.send(gu_sum.at[p, far], gu_far.at[p], me.at(zh=1))
        add_cores(me, p, me.zh, gu, gu_in, gu_sum)

    def send_hidden(p):
        arrive([across[p]])
        activate(me, p, gu_sum, gu_far, blocks)
        own = blocks.at[pl.ds(2 * p, 2), me.zh, me.c]
        across[p] = wire.send(own, own, me.at(zh=1))

    def send_pair(p):
        arrive([across[p]])
        pair = blocks.at[pl.ds(2 * p, 2), :, me.c]
        near[p] = wire.send(pair, pair, me.at(c=1))

    arrive(lines[0] + lines[1])
    normalise(me, 0, every, known, gain, normed)
    gate_up_products(0, normed, wg, wu, gu)
    send_core(0)
    qkv_products(0, normed, wq, qkv)
    send_far(0)
    arrive(lines[2] + lines[3])
    normalise(me, 1, every, known, gain, normed)
    qkv_products(1, normed, wq, qkv)

    def qkv_piece(c, d):
        return qkv.at[(me.x + d - me.z + 4) % 4, :, (me.c + c) % 2]

    copies = two_way(me, wire, "x", "c", qkv_piece, s1)
    s1[0, me.x] = qkv[(me.x - me.z + 4) % 4, :, me.c]
    gate_up_products(1, normed, wg, wu, gu)
    send_core(1)
    arrive(copies)
    mixed = (s1[0].astype(F32) + s1[1].astype(F32)).reshape(4, 2, 4, 8, 128)
    for h in range(2):
        for t in range(4):
            q2[h, t] = mixed[:, h, t].reshape(32, 128).astype(BF16)
    copies = two_way(
        me, wire, "z", "zh", lambda h, d: q2.at[(me.zh + h) % 2, (me.z + d) % 4], s2
    )
    s2[0, me.z] = q2[me.zh, me.z]
    send_far(1)
    arrive(copies)
    s2_sum[...] = (s2[0].astype(F32) + s2[1].astype(F32)).astype(BF16)
    copies = [wire.send(s2_sum, s3.at[me.y], me.at(y=d)) for d in (1, 2, 3)]
    s3[me.y] = s2_sum[...]
    loads[5].wait()
    arrive(copies)
    g_ref[...] = dot(pick_in[...], s3[...].reshape(512, 128))
    attend(lengths_ref[0], g_ref, cache, t_ref, flat, heads32, fresh_v, flat_out, t_wide)

    copies = two_way(me, wire, "x", "c", lambda c, d: t_ref.at[(me.x + d) % 4], u1)
    u1[0, me.x] = t_ref[me.x]
    send_hidden(0)
    arrive(copies)
    mixed = u1[...].astype(F32).reshape(8, 4, 8, 128)
    for t in range(4):
        u1_sorted[t] = mixed[:, t].reshape(64, 128).astype(BF16)
    copies = two_way(me, wire, "z", "zh", lambda h, d: u1_sorted.at[(me.z + d) % 4], u2)
    u2[0, me.z] = u1_sorted[me.z]
    send_hidden(1)
    send_pair(0)
    arrive(copies)
    u2_sorted[...] = (
        dot(pick_mid[...], u2[...].reshape(512, 128)).astype(BF16).reshape(4, 128, 128)
    )
    copies = [
        wire.send(u2_sorted.at[(me.y + d) % 4], u3.at[me.y], me.at(y=d)) for d in (1, 2, 3)
    ]
    u3[me.y] = u2_sorted[me.y]
    for i in (6, 7):
        loads[i].wait()
    arrive(copies)
    heads[...] = dot(pick_out[...], u3[...].reshape(512, 128)).astype(BF16)

    def send_rows(e):
        copies = []
        for d in (1, 2, 3):
            if last_axis[e] == "y":
                src = partial.at[e, :, (me.y + d) % 4]
            else:
                src = partial.at[e, (me.x + d) % 4]
            copies.append(wire.send(src, ra.at[e, d - 1], me.at(**{last_axis[e]: d})))
        return copies

    def send_row(e, copies):
        arrive(copies)

        def body(i, _):
            if last_axis[e] == "y":
                total = partial[e, i, me.y].astype(F32)
            else:
                total = partial[e, me.x, i].astype(F32)
            for d in range(3):
                total = total + ra[e, d, i].astype(F32)
            sa[e, i] = total.astype(BF16)
            return 0

        lax.fori_loop(0, 4, body, 0)
        here = getattr(me, first_axis[e])
        return [
            wire.send(sa.at[e, (here + d) % 4], rb.at[e, d - 1], me.at(**{first_axis[e]: d}))
            for d in (1, 2, 3)
        ]

    def row_sum(e, copies):
        arrive(copies)
        total = sa[e, getattr(me, first_axis[e])].astype(F32)
        for d in range(3):
            total = total + rb[e, d].astype(F32)
        return total

    def send_block(e, copies):
        sz[e - 1] = row_sum(e, copies).astype(BF16)
        return wire.send(sz.at[e - 1], rz.at[e - 1], me.at(z=e))

    rows = {}
    arrive([near[0]])
    second_products(0, blocks, heads, wo, wd, partial)
    rows[1] = send_rows(1)
    rows[0] = send_rows(0)
    send_pair(1)
    arrive([near[1]])
    second_products(1, blocks, heads, wo, wd, partial)
    rows[2] = send_rows(2)
    rows[3] = send_rows(3)
    row = {1: send_row(1, rows[1])}
    row[0] = send_row(0, rows[0])
    row[2] = send_row(2, rows[2])
    ends = [send_block(1, row[1])]
    row[3] = send_row(3, rows[3])
    ends.append(send_block(2, row[2]))
    total = row_sum(0, row[0])
    ends.append(send_block(3, row[3]))
    arrive(ends)
    for e in range(3):
        total = total + rz[e].astype(F32)
    whole = jnp.concatenate([total[:8], total[8:]], 1)
    for step in range(STEPS):
        out_ref[step] = (
            hidden[step].astype(F32) + whole[4 * step : 4 * step + 4]
        ).astype(BF16)
    wire.close()


def per_device(hidden_in, norm_gain, w_qkv, w_gate, w_up, w_out, w_down, kv_cache, lengths):
    far = pl.BlockSpec(memory_space=pltpu.HBM)
    scratch = [
        ((2, 4, WIDTH), BF16), ((1, WIDTH), F32), ((QCOLS, WIDTH), BF16), ((UNITS, WIDTH), BF16),
        ((UNITS, WIDTH), BF16), ((OCOLS, WIDTH), BF16), ((UNITS, WIDTH), BF16),
        ((1, CTX, 512), BF16), 8,
        ((4, 2, 8, 128), F32), ((4, 4, 4, 8, 128), F32), ((4, 4, 4, 16, HALF), BF16),
        ((512, WIDTH), BF16), ((4, 2, 2, 32, 128), BF16), ((4, 2, 2, 32, HALF), BF16),
        ((2, 2, 2, 32, HALF), BF16), ((2, 2, 2, 32, HALF), BF16), ((2, 2, 32, HALF), BF16),
        ((4, 2, 2, 32, 640), BF16),
        ((2, 4, 2, 32, 128), BF16), ((2, 4, 32, 128), BF16), ((2, 4, 32, 128), BF16),
        ((4, 32, 128), BF16), ((4, 4, 32, 128), BF16), ((128, 128), F32), ((4, 32, 128), BF16),
        ((2, 6656), F32), ((56, 256), F32), ((16, 256), F32), ((2, 6144), F32), ((128, 128), F32),
        ((2, 4, 32, 128), BF16), ((4, 64, 128), BF16), ((2, 4, 64, 128), BF16),
        ((4, 128, 128), BF16), ((4, 128, 128), BF16), ((512, 128), BF16),
        ((128, 512), BF16), ((512, 512), BF16), ((512, 512), BF16),
        ((4, 4, 4, 16, HALF), BF16), ((4, 3, 4, 16, HALF), BF16), ((4, 4, 16, HALF), BF16),
        ((4, 3, 16, HALF), BF16), ((3, 16, HALF), BF16), ((3, 16, HALF), BF16),
        128, 128,
    ]
    return pl.pallas_call(
        kernel,
        name="layer",
        out_shape=jax.ShapeDtypeStruct((2, 4, WIDTH), BF16),
        in_specs=[pl.BlockSpec(memory_space=pltpu.SMEM)] + [far] * 8,
        out_specs=pl.BlockSpec(memory_space=pltpu.VMEM),
        scratch_shapes=[
            pltpu.SemaphoreType.DMA((entry,)) if isinstance(entry, int) else pltpu.VMEM(*entry)
            for entry in scratch
        ],
        compiler_params=pltpu.CompilerParams(
            collective_id=0, has_side_effects=True, vmem_limit_bytes=56 * 2**20
        ),
    )(
        lengths, hidden_in, norm_gain.reshape(1, WIDTH), w_qkv.T, w_gate.T, w_up.T,
        w_out, w_down, kv_cache,
    )


def solution(mesh):
    return jax.shard_map(
        per_device,
        mesh=mesh,
        in_specs=(
            P(None, "yz", "gx"),
            P("gx"),
            P("gx", "yz"),
            P("gx", "yz"),
            P("gx", "yz"),
            P("yz", "gx"),
            P("yz", "gx"),
            P(("gx", "yz"), None, None),
            P(("gx", "yz")),
        ),
        out_specs=P(None, "yz", "gx"),
        check_vma=False,
    )
```

time: 1640 us -> 117 us (0.07); the launches traced: 1610 us -> 116 us
  waiting for transfers between devices: 1460 us -> 0 us
  Pallas kernels: 0 us -> 113 us
  starting transfers between devices: 42 us -> 0 us
  blocking collectives: 41.4 us -> 0 us
  matrix products: 34.9 us -> 0 us
    unnamed x7 -> x0, waiting for transfers between devices: 692 us -> none
    all_gather x2 -> x0, waiting for transfers between devices: 645 us -> none  [per_device(): every_row = lax.all_gather(normed, 'yz', axis=0, tiled=True)]
    pallas_call x0 -> x1, Pallas kernels: none -> 113 us  [per_device(): pl.pallas_call(kernel, name='layer', out_shape=jax.ShapeDtypeStruct((2, 4...]
    reduce_scatter x2 -> x0, waiting for transfers between devices: 81.3 us -> none  [per_device(): lax.psum_scatter(jnp.dot(every_row, w_qkv, preferred_element_type=jnp.flo...]
    all_to_all x4 -> x0, starting transfers between devices: 41.7 us -> none  [the longest x2 25.3 us: per_device(): lax.all_to_all(attended, 'yz', split_axis=1, concat_axis=0, tiled=True)]
    dot_general x17 -> x0, matrix products: 34.9 us -> none  [the longest x2 7.86 us: per_device(): jnp.dot(every_row, w_gate, preferred_element_type=jnp.float32)]
    all_gather x2 -> x0, blocking collectives: 24.9 us -> none  [per_device(): head_rows = lax.all_gather(head_block, 'gx', axis=0, tiled=True)]
    all_to_all x4 -> x0, waiting for transfers between devices: 23 us -> none  [the longest x2 13.9 us: per_device(): lax.all_to_all(attended, 'yz', split_axis=1, concat_axis=0, tiled=True)]
  transfers between devices with their start and end apart: 10 -> 0, of which waited for: 9 -> 0; matrix products, arithmetic and copies ran while one was open for 2% -> 0% of each run, Pallas kernels for 0% -> 0%
where the time goes in v2:
time: 117 us; the launch traced here: 116 us
  Pallas kernels  113 us (97%)
  local copies, waits for them, and re-layouts  2.71 us (2%)
    pallas_call x1, Pallas kernels, per_device(): pl.pallas_call(kernel, name='layer', out_shape=jax.ShapeDtypeStruct((2, 4...  113 us

profile of v2, /device:TPU:2, one launch (start us, length us, event | category | flops | bytes accessed | tf_op | source)
XLA Modules:
  0.0 115.9 jit_solution(4383669116610010805)
XLA Ops:
  0.7 1.3 %reshape.3.gain_hbm = f32[1,2304]{1,0:T(1,128)} reshape(f32[2304]{0:T(1024)} %param.10) | data formatting | bytes 18432 | tf_op jit(solution)/shard_map/reshape | solution.py:519
  2.0 112.6 %layer.1 = bf16[2,4,2304]{2,1,0:T(4,128)(2,1)} custom-call(s32[1]{0:T(128)S(6)} %copy.11.lengths_ref, bf16[2,4,2304]{2,1,0:T(4,128)(2,1)} %hidden_hbm.1, f32[1,2304]{1,0:T(1,128)} %reshape.3.gain_hbm, bf16[104,2304]{1,0:T(8,128)(2,1)} %bitcast.5, bf16[576,2304]{1,0:T(8,128)(2,1)} %bitcast.3, bf16[576,2304]{1,0:T(8,128)(2,1)} %bitcast.4, ...), custom_call_target="tpu_custom_call" | custom-call | tf_op jit(solution)/shard_map/layer/pallas_call | solution.py:505
  114.5 1.4 %copy.12 = bf16[2,4,2304]{2,1,0:T(4,128)(2,1)} copy(bf16[2,4,2304]{2,1,0:T(4,128)(2,1)} %layer.1) | data formatting | bytes 73728

commit v3 on v2

--- a/solution.py
+++ b/solution.py
@@ -41,7 +41,8 @@
     count = 0
     for d in (1, 2, 3):
         partners = [me.at(x=d), me.at(z=d), me.at(y=d), me.at(c=1, x=d), me.at(zh=1, z=d)]
-        partners.append(me.at(zh=d // 2, c=d % 2))
+        if d < 3:
+            partners.append(me.at(zh=d // 2, c=d % 2))
         for target in partners:
             pl.semaphore_signal(barrier, inc=1, device_id=target, device_id_type=MESH)
             count += 1
@@ -86,35 +87,41 @@
     return lax.dot_general(a, b, (((1,), (1,)), ((), ())), preferred_element_type=F32)
 
 
-def fold(hidden, own, stats):
+def fold(hidden, own, part):
     rows = jnp.concatenate([hidden[0].astype(F32), hidden[1].astype(F32)], 0)
     own[...] = jnp.concatenate([rows[:, :HALF], rows[:, HALF:]], 0).astype(BF16)
-    stats[0, 0] = jnp.broadcast_to(jnp.sum(rows, 1, keepdims=True), (8, 128))
-    stats[0, 1] = jnp.broadcast_to(jnp.sum(rows * rows, 1, keepdims=True), (8, 128))
-
-
-def moments(stats):
-    total = (stats[0] + stats[1]) + (stats[2] + stats[3])
-    mean = total[0] / D
-    var = total[1] / D - mean * mean
     lane = lax.broadcasted_iota(jnp.int32, (8, 128), 1)
-    return jnp.where(lane < 64, mean, lax.rsqrt(var + EPS))
-
-
-def normalise(me, p, every, known, gain, normed):
+    sums = jnp.sum(rows, 1, keepdims=True)
+    squares = jnp.sum(rows * rows, 1, keepdims=True)
+    part[...] = jnp.where(lane < 64, sums, squares)
+
+
+def normalise(me, raw, sums, gain, every):
+    def body(z, _):
+        total = (sums[0, z] + sums[1, z]) / D
+        mean = total[:, :1]
+        var = total[:, 64:65] - mean * mean
+        scale = lax.rsqrt(var + EPS)
+        block = raw[z].astype(F32)
+        left = (block[:8] - mean) * scale * gain[:, :HALF]
+        right = (block[8:] - mean) * scale * gain[:, HALF:]
+        every[z, me.x, me.y] = jnp.concatenate([left, right], 0).astype(BF16)
+        return 0
+
+    lax.fori_loop(0, 4, body, 0)
+
+
+def unfold(me, e, every, normed):
+    z = (me.z + e) % 4
+
     def body(i, _):
-        z = (me.z + 2 * p + i // 4) % 4
-        block = every[z, i % 4].astype(F32)
-        about = known[i % 4, z].reshape(32, 128)
-        mean, scale = about[:, :1], about[:, 64:65]
-        left = (block[:, :8].reshape(32, HALF) - mean) * scale * gain[:, :HALF]
-        right = (block[:, 8:].reshape(32, HALF) - mean) * scale * gain[:, HALF:]
-        rows = pl.ds(pl.multiple_of(p * 256 + i * 32, 32), 32)
-        normed[rows, :HALF] = left.astype(BF16)
-        normed[rows, HALF:] = right.astype(BF16)
+        block = every[z, i].astype(F32)
+        rows = pl.ds(pl.multiple_of(e * 128 + i * 32, 32), 32)
+        normed[rows, :HALF] = block[:, :8].reshape(32, HALF).astype(BF16)
+        normed[rows, HALF:] = block[:, 8:].reshape(32, HALF).astype(BF16)
         return 0
 
-    lax.fori_loop(0, 8, body, 0)
+    lax.fori_loop(0, 4, body, 0)
 
 
 def qkv_products(p, normed, wq, qkv):
@@ -249,18 +256,22 @@
     write(pick_out, by_row, lambda k: k >= 0)
 
 
-def second_products(p, blocks, heads, wo, wd, partial):
+def down_products(p, blocks, wd, early):
     lines = blocks[2 * p : 2 * p + 2].reshape(256, 640)
+    for n in range(0, WIDTH, 384):
+        columns = slice(n, n + 384)
+        early[:, columns] = dot(lines[:, :512], wd[:512, columns]) + dot(
+            lines[:, 512:UNITS], wd[512:, columns]
+        )
+
+
+def out_products(p, early, heads, wo, partial):
     attended = heads[256 * p : 256 * p + 256, :OCOLS]
     for n in range(0, HALF, 384):
         sides = []
         for at in (n, HALF + n):
             columns = slice(at, at + 384)
-            product = (
-                dot(lines[:, :512], wd[:512, columns])
-                + dot(lines[:, 512:UNITS], wd[512:, columns])
-                + dot(attended, wo[:, columns])
-            )
+            product = early[:, columns] + dot(attended, wo[:, columns])
             sides.append(product.reshape(2, 4, 4, 8, 384))
         partial[2 * p : 2 * p + 2, :, :, :, n : n + 384] = jnp.concatenate(sides, 3).astype(BF16)
 
@@ -268,10 +279,10 @@
 def kernel(
     lengths_ref, hidden_hbm, gain_hbm, wq_hbm, wg_hbm, wu_hbm, wo_hbm, wd_hbm, cache_hbm, out_ref,
     hidden, gain, wq, wg, wu, wo, wd, cache, load_sems,
-    stats, known, every, normed, qkv, gu, gu_in, gu_sum, gu_far, blocks,
+    part, part_in, pair, sums, raw, every, normed, qkv, gu, gu_in, gu_sum, gu_far, blocks,
     s1, q2, s2, s2_sum, s3, g_ref, t_ref, flat, heads32, fresh_v, flat_out, t_wide,
     u1, u1_sorted, u2, u2_sorted, u3, heads, pick_in, pick_mid, pick_out,
-    partial, ra, sa, rb, sz, rz,
+    early, partial, ra, sa, rb, sz, rz,
     send_sems, recv_sems,
 ):
     me = Place()
@@ -279,14 +290,14 @@
     loads = []
     for i, (src, dst) in enumerate(
         (
-            (hidden_hbm, hidden), (gain_hbm, gain), (wq_hbm, wq), (wg_hbm, wg),
+            (hidden_hbm, hidden), (gain_hbm, gain.at[0]), (wq_hbm, wq), (wg_hbm, wg),
             (wu_hbm, wu), (cache_hbm, cache), (wo_hbm, wo), (wd_hbm, wd),
         )
     ):
         loads.append(pltpu.make_async_copy(src, dst, load_sems.at[i]))
         loads[-1].start()
     loads[0].wait()
-    fold(hidden, every.at[me.z, me.x, me.y], stats)
+    fold(hidden, raw.at[me.z], part)
     greet(me)
 
     first_axis = ("x", "y", "x", "y")
@@ -302,31 +313,29 @@
         line = every.at[z, :, me.y] if first_axis[e] == "x" else every.at[z, me.x]
         return [wire.send(line, line, me.at(**{last_axis[e]: d})) for d in (1, 2, 3)]
 
-    own = every.at[me.z, me.x, me.y]
-    sums = [wire.send(stats.at[0], stats.at[d], me.at(zh=d // 2, c=d % 2)) for d in (1, 2, 3)]
+    swap = wire.send(part, part_in, me.at(c=1))
+    own = raw.at[me.z]
     shards = [wire.send(own, own, me.at(z=d)) for d in (1, 2, 3)]
-    owns = [send_own(0)]
+    arrive([swap])
+    pair[...] = part[...] + part_in[...]
+    sums[0, me.z] = pair[...]
+    facts = two_way(me, wire, "z", "zh", lambda h, d: pair, sums)
+    write_picks(me, pick_in, pick_mid, pick_out)
+    loads[1].wait()
     arrive(shards)
-    owns += [send_own(e) for e in (1, 2, 3)]
-    arrive(owns[0])
-    lines = [send_line(0)]
-    arrive(sums)
-    known[me.x, me.z, me.y] = moments(stats)
-    mine = known.at[me.x, me.z, me.y]
-    facts = [wire.send(mine, mine, me.at(z=d)) for d in (1, 2, 3)]
-    for e in (1, 2, 3):
+    arrive(facts)
+    normalise(me, raw, sums, gain, every)
+    owns, lines = [send_own(e) for e in range(4)], [None] * 4
+    for e in (0, 1):
         arrive(owns[e])
-        lines.append(send_line(e))
-    arrive(facts)
-    mine = known.at[me.x, :, me.y]
-    facts = [wire.send(mine, mine, me.at(x=d)) for d in (1, 2, 3)]
-    write_picks(me, pick_in, pick_mid, pick_out)
-    arrive(facts)
-    mine = known.at[:, :, me.y]
-    facts = [wire.send(mine, mine, me.at(y=d)) for d in (1, 2, 3)]
-    for i in (1, 2, 3, 4):
+        lines[e] = send_line(e)
+    for i in (2, 3, 4):
         loads[i].wait()
-    arrive(facts)
+    arrive(owns[2] + owns[3])
+    for e in (0, 1):
+        arrive(lines[e])
+        lines[e + 2] = send_line(e + 2)
+        unfold(me, e, every, normed)
 
     far = 1 - me.zh
     near, across = [None, None], [None, None]
@@ -352,14 +361,13 @@
         pair = blocks.at[pl.ds(2 * p, 2), :, me.c]
         near[p] = wire.send(pair, pair, me.at(c=1))
 
-    arrive(lines[0] + lines[1])
-    normalise(me, 0, every, known, gain, normed)
     gate_up_products(0, normed, wg, wu, gu)
     send_core(0)
     qkv_products(0, normed, wq, qkv)
     send_far(0)
-    arrive(lines[2] + lines[3])
-    normalise(me, 1, every, known, gain, normed)
+    for e in (2, 3):
+        arrive(lines[e])
+        unfold(me, e, every, normed)
     qkv_products(1, normed, wq, qkv)
 
     def qkv_piece(c, d):
@@ -383,6 +391,7 @@
     s2_sum[...] = (s2[0].astype(F32) + s2[1].astype(F32)).astype(BF16)
     copies = [wire.send(s2_sum, s3.at[me.y], me.at(y=d)) for d in (1, 2, 3)]
     s3[me.y] = s2_sum[...]
+    send_hidden(0)
     loads[5].wait()
     arrive(copies)
     g_ref[...] = dot(pick_in[...], s3[...].reshape(512, 128))
@@ -390,7 +399,7 @@
 
     copies = two_way(me, wire, "x", "c", lambda c, d: t_ref.at[(me.x + d) % 4], u1)
     u1[0, me.x] = t_ref[me.x]
-    send_hidden(0)
+    send_pair(0)
     arrive(copies)
     mixed = u1[...].astype(F32).reshape(8, 4, 8, 128)
     for t in range(4):
@@ -398,7 +407,6 @@
     copies = two_way(me, wire, "z", "zh", lambda h, d: u1_sorted.at[(me.z + d) % 4], u2)
     u2[0, me.z] = u1_sorted[me.z]
     send_hidden(1)
-    send_pair(0)
     arrive(copies)
     u2_sorted[...] = (
         dot(pick_mid[...], u2[...].reshape(512, 128)).astype(BF16).reshape(4, 128, 128)
@@ -409,6 +417,9 @@
     u3[me.y] = u2_sorted[me.y]
     for i in (6, 7):
         loads[i].wait()
+    arrive([near[0]])
+    down_products(0, blocks, wd, early)
+    send_pair(1)
     arrive(copies)
     heads[...] = dot(pick_out[...], u3[...].reshape(512, 128)).astype(BF16)
 
@@ -454,13 +465,12 @@
         return wire.send(sz.at[e - 1], rz.at[e - 1], me.at(z=e))
 
     rows = {}
-    arrive([near[0]])
-    second_products(0, blocks, heads, wo, wd, partial)
+    out_products(0, early, heads, wo, partial)
     rows[1] = send_rows(1)
     rows[0] = send_rows(0)
-    send_pair(1)
     arrive([near[1]])
-    second_products(1, blocks, heads, wo, wd, partial)
+    down_products(1, blocks, wd, early)
+    out_products(1, early, heads, wo, partial)
     rows[2] = send_rows(2)
     rows[3] = send_rows(3)
     row = {1: send_row(1, rows[1])}
@@ -488,7 +498,8 @@
         ((2, 4, WIDTH), BF16), ((1, WIDTH), F32), ((QCOLS, WIDTH), BF16), ((UNITS, WIDTH), BF16),
         ((UNITS, WIDTH), BF16), ((OCOLS, WIDTH), BF16), ((UNITS, WIDTH), BF16),
         ((1, CTX, 512), BF16), 8,
-        ((4, 2, 8, 128), F32), ((4, 4, 4, 8, 128), F32), ((4, 4, 4, 16, HALF), BF16),
+        ((8, 128), F32), ((8, 128), F32), ((8, 128), F32), ((2, 4, 8, 128), F32),
+        ((4, 16, HALF), BF16), ((4, 4, 4, 16, HALF), BF16),
         ((512, WIDTH), BF16), ((4, 2, 2, 32, 128), BF16), ((4, 2, 2, 32, HALF), BF16),
         ((2, 2, 2, 32, HALF), BF16), ((2, 2, 2, 32, HALF), BF16), ((2, 2, 32, HALF), BF16),
         ((4, 2, 2, 32, 640), BF16),
@@ -498,7 +509,7 @@
         ((2, 4, 32, 128), BF16), ((4, 64, 128), BF16), ((2, 4, 64, 128), BF16),
         ((4, 128, 128), BF16), ((4, 128, 128), BF16), ((512, 128), BF16),
         ((128, 512), BF16), ((512, 512), BF16), ((512, 512), BF16),
-        ((4, 4, 4, 16, HALF), BF16), ((4, 3, 4, 16, HALF), BF16), ((4, 4, 16, HALF), BF16),
+        ((256, WIDTH), F32), ((4, 4, 4, 16, HALF), BF16), ((4, 3, 4, 16, HALF), BF16), ((4, 4, 16, HALF), BF16),
         ((4, 3, 16, HALF), BF16), ((3, 16, HALF), BF16), ((3, 16, HALF), BF16),
         128, 128,
     ]
@@ -516,7 +527,7 @@
             collective_id=0, has_side_effects=True, vmem_limit_bytes=56 * 2**20
         ),
     )(
-        lengths, hidden_in, norm_gain.reshape(1, WIDTH), w_qkv.T, w_gate.T, w_up.T,
+        lengths, hidden_in, norm_gain, w_qkv.T, w_gate.T, w_up.T,
         w_out, w_down, kv_cache,
     )
 

time: 117 us -> 103 us (0.88)
  Pallas kernels: 113 us -> 101 us
  local copies, waits for them, and re-layouts: 2.71 us -> 1.4 us
    pallas_call x1, Pallas kernels: 113 us -> 101 us  [per_device(): pl.pallas_call(kernel, name='layer', out_shape=jax.ShapeDtypeStruct((2, 4...]
    reshape x1 -> x0, local copies, waits for them, and re-layouts: 1.31 us -> none  [per_device(): norm_gain.reshape(1, WIDTH)]
where the time goes in v3:
time: 103 us
  Pallas kernels  101 us (98%)
  local copies, waits for them, and re-layouts  1.4 us (1%)
    pallas_call x1, Pallas kernels, per_device(): pl.pallas_call(kernel, name='layer', out_shape=jax.ShapeDtypeStruct((2, 4...  101 us

profile of v3, /device:TPU:2, one launch (start us, length us, event | category | flops | bytes accessed | tf_op | source)
XLA Modules:
  0.0 102.8 jit_solution(4867215467829877524)
XLA Ops:
  0.7 100.7 %layer.1 = bf16[2,4,2304]{2,1,0:T(4,128)(2,1)} custom-call(s32[1]{0:T(128)S(6)} %copy.11.lengths_ref, bf16[2,4,2304]{2,1,0:T(4,128)(2,1)} %hidden_hbm.1, f32[2304]{0:T(1024)} %gain_hbm.1, bf16[104,2304]{1,0:T(8,128)(2,1)} %bitcast.5, bf16[576,2304]{1,0:T(8,128)(2,1)} %bitcast.3, bf16[576,2304]{1,0:T(8,128)(2,1)} %bitcast.4, bf16[96,2304]{1,0:T(8,128)(2,1)} %wo_hbm.1, ...), custom_call_target="tpu_custom_call" | custom-call | tf_op jit(solution)/shard_map/layer/pallas_call | solution.py:516
  101.4 1.4 %copy.12 = bf16[2,4,2304]{2,1,0:T(4,128)(2,1)} copy(bf16[2,4,2304]{2,1,0:T(4,128)(2,1)} %layer.1) | data formatting | bytes 73728

commit v4 on v3

--- a/solution.py
+++ b/solution.py
@@ -46,7 +46,7 @@
         for target in partners:
             pl.semaphore_signal(barrier, inc=1, device_id=target, device_id_type=MESH)
             count += 1
-    pl.semaphore_wait(barrier, count)
+    return count
 
 
 class Wire:
@@ -124,41 +124,38 @@
     lax.fori_loop(0, 4, body, 0)
 
 
-def qkv_products(p, normed, wq, qkv):
-    part = dot_t(normed[256 * p : 256 * p + 256, :], wq[...])
-    part = jnp.concatenate([part, jnp.zeros((256, 24), F32)], 1)
-    qkv[2 * p : 2 * p + 2] = part.reshape(2, 2, 2, 32, 128).astype(BF16)
-
-
-def gate_up_products(p, normed, wg, wu, gu):
-    rows = normed[256 * p : 256 * p + 256, :]
+def qkv_products(first, planes, normed, wq, qkv):
+    rows = 128 * planes
+    part = dot_t(normed[128 * first : 128 * first + rows, :], wq[...])
+    part = jnp.concatenate([part, jnp.zeros((rows, 24), F32)], 1)
+    qkv[first : first + planes] = part.reshape(planes, 2, 2, 32, 128).astype(BF16)
+
+
+def gate_up_products(e, normed, wg, wu, gu):
+    rows = normed[128 * e : 128 * e + 128, :]
     gate = dot_t(rows, wg[...])
     up = dot_t(rows, wu[...])
     tail = jnp.concatenate([gate[:, 512:], up[:, 512:]], 1)
-    own = slice(2 * p, 2 * p + 2)
-    gu[own, :, :, :, :512] = gate[:, :512].reshape(2, 2, 2, 32, 512).astype(BF16)
-    gu[own, :, :, :, 512:1024] = up[:, :512].reshape(2, 2, 2, 32, 512).astype(BF16)
-    gu[own, :, :, :, 1024:] = tail.reshape(2, 2, 2, 32, 128).astype(BF16)
-
-
-def add_cores(me, p, half, gu, gu_in, gu_sum):
-    def body(e, _):
-        total = gu[2 * p + e, half, me.c].astype(F32) + gu_in[p, e, half].astype(F32)
-        gu_sum[p, half, e] = total.astype(BF16)
-        return 0
-
-    lax.fori_loop(0, 2, body, 0)
+    gu[e, :, :, :, :512] = gate[:, :512].reshape(2, 2, 32, 512).astype(BF16)
+    gu[e, :, :, :, 512:1024] = up[:, :512].reshape(2, 2, 32, 512).astype(BF16)
+    gu[e, :, :, :, 1024:] = tail.reshape(2, 2, 32, 128).astype(BF16)
+
+
+def add_cores(me, e, half, gu, gu_in, gu_sum):
+    total = gu[e, half, me.c].astype(F32) + gu_in[e, half].astype(F32)
+    gu_sum[e, half] = total.astype(BF16)
 
 
 def activate(me, p, gu_sum, gu_far, blocks):
-    def body(e, _):
-        total = gu_sum[p, me.zh, e].astype(F32) + gu_far[p, e].astype(F32)
+    def body(i, _):
+        e = 2 * p + i
+        total = gu_sum[e, me.zh].astype(F32) + gu_far[e].astype(F32)
         gate, up = total[:, :512], total[:, 512:1024]
         tail = total[:, 1024:]
         last = tail / (1.0 + jnp.exp(-tail)) * pltpu.roll(tail, 64, 1)
         lane = lax.broadcasted_iota(jnp.int32, last.shape, 1)
-        blocks[2 * p + e, me.zh, me.c, :, :512] = (gate / (1.0 + jnp.exp(-gate)) * up).astype(BF16)
-        blocks[2 * p + e, me.zh, me.c, :, 512:] = jnp.where(lane < 64, last, 0.0).astype(BF16)
+        blocks[e, me.zh, me.c, :, :512] = (gate / (1.0 + jnp.exp(-gate)) * up).astype(BF16)
+        blocks[e, me.zh, me.c, :, 512:] = jnp.where(lane < 64, last, 0.0).astype(BF16)
         return 0
 
     lax.fori_loop(0, 2, body, 0)
@@ -282,7 +279,7 @@
     part, part_in, pair, sums, raw, every, normed, qkv, gu, gu_in, gu_sum, gu_far, blocks,
     s1, q2, s2, s2_sum, s3, g_ref, t_ref, flat, heads32, fresh_v, flat_out, t_wide,
     u1, u1_sorted, u2, u2_sorted, u3, heads, pick_in, pick_mid, pick_out,
-    early, partial, ra, sa, rb, sz, rz,
+    early, partial, ra, relay, sa, rb, sz, rz,
     send_sems, recv_sems,
 ):
     me = Place()
@@ -296,9 +293,10 @@
     ):
         loads.append(pltpu.make_async_copy(src, dst, load_sems.at[i]))
         loads[-1].start()
+    count = greet(me)
     loads[0].wait()
     fold(hidden, raw.at[me.z], part)
-    greet(me)
+    pl.semaphore_wait(pltpu.get_barrier_semaphore(), count)
 
     first_axis = ("x", "y", "x", "y")
     last_axis = ("y", "x", "y", "x")
@@ -332,26 +330,21 @@
     for i in (2, 3, 4):
         loads[i].wait()
     arrive(owns[2] + owns[3])
-    for e in (0, 1):
-        arrive(lines[e])
-        lines[e + 2] = send_line(e + 2)
-        unfold(me, e, every, normed)
 
     far = 1 - me.zh
-    near, across = [None, None], [None, None]
-
-    def send_core(p):
-        src = gu.at[pl.ds(2 * p, 2), :, 1 - me.c]
-        near[p] = wire.send(src, gu_in.at[p], me.at(c=1))
-
-    def send_far(p):
-        arrive([near[p]])
-        add_cores(me, p, far, gu, gu_in, gu_sum)
-        across[p] = wire.send(gu_sum.at[p, far], gu_far.at[p], me.at(zh=1))
-        add_cores(me, p, me.zh, gu, gu_in, gu_sum)
+    near, across = [None] * 4, [None] * 4
+
+    def send_core(e):
+        near[e] = wire.send(gu.at[e, :, 1 - me.c], gu_in.at[e], me.at(c=1))
+
+    def send_far(e):
+        arrive([near[e]])
+        add_cores(me, e, far, gu, gu_in, gu_sum)
+        across[e] = wire.send(gu_sum.at[e, far], gu_far.at[e], me.at(zh=1))
+        add_cores(me, e, me.zh, gu, gu_in, gu_sum)
 
     def send_hidden(p):
-        arrive([across[p]])
+        arrive(across[2 * p : 2 * p + 2])
         activate(me, p, gu_sum, gu_far, blocks)
         own = blocks.at[pl.ds(2 * p, 2), me.zh, me.c]
         across[p] = wire.send(own, own, me.at(zh=1))
@@ -361,22 +354,36 @@
         pair = blocks.at[pl.ds(2 * p, 2), :, me.c]
         near[p] = wire.send(pair, pair, me.at(c=1))
 
+    arrive(lines[0])
+    lines[2] = send_line(2)
+    unfold(me, 0, every, normed)
     gate_up_products(0, normed, wg, wu, gu)
     send_core(0)
-    qkv_products(0, normed, wq, qkv)
+    arrive(lines[1])
+    lines[3] = send_line(3)
+    unfold(me, 1, every, normed)
     send_far(0)
-    for e in (2, 3):
-        arrive(lines[e])
-        unfold(me, e, every, normed)
-    qkv_products(1, normed, wq, qkv)
+    gate_up_products(1, normed, wg, wu, gu)
+    send_core(1)
+    qkv_products(0, 2, normed, wq, qkv)
+    send_far(1)
+    arrive(lines[2])
+    unfold(me, 2, every, normed)
+    gate_up_products(2, normed, wg, wu, gu)
+    send_core(2)
+    qkv_products(2, 1, normed, wq, qkv)
+    send_far(2)
+    arrive(lines[3])
+    unfold(me, 3, every, normed)
+    qkv_products(3, 1, normed, wq, qkv)
 
     def qkv_piece(c, d):
         return qkv.at[(me.x + d - me.z + 4) % 4, :, (me.c + c) % 2]
 
     copies = two_way(me, wire, "x", "c", qkv_piece, s1)
     s1[0, me.x] = qkv[(me.x - me.z + 4) % 4, :, me.c]
-    gate_up_products(1, normed, wg, wu, gu)
-    send_core(1)
+    gate_up_products(3, normed, wg, wu, gu)
+    send_core(3)
     arrive(copies)
     mixed = (s1[0].astype(F32) + s1[1].astype(F32)).reshape(4, 2, 4, 8, 128)
     for h in range(2):
@@ -386,11 +393,11 @@
         me, wire, "z", "zh", lambda h, d: q2.at[(me.zh + h) % 2, (me.z + d) % 4], s2
     )
     s2[0, me.z] = q2[me.zh, me.z]
-    send_far(1)
     arrive(copies)
     s2_sum[...] = (s2[0].astype(F32) + s2[1].astype(F32)).astype(BF16)
     copies = [wire.send(s2_sum, s3.at[me.y], me.at(y=d)) for d in (1, 2, 3)]
     s3[me.y] = s2_sum[...]
+    send_far(3)
     send_hidden(0)
     loads[5].wait()
     arrive(copies)
@@ -399,6 +406,7 @@
 
     copies = two_way(me, wire, "x", "c", lambda c, d: t_ref.at[(me.x + d) % 4], u1)
     u1[0, me.x] = t_ref[me.x]
+    send_hidden(1)
     send_pair(0)
     arrive(copies)
     mixed = u1[...].astype(F32).reshape(8, 4, 8, 128)
@@ -406,7 +414,6 @@
         u1_sorted[t] = mixed[:, t].reshape(64, 128).astype(BF16)
     copies = two_way(me, wire, "z", "zh", lambda h, d: u1_sorted.at[(me.z + d) % 4], u2)
     u2[0, me.z] = u1_sorted[me.z]
-    send_hidden(1)
     arrive(copies)
     u2_sorted[...] = (
         dot(pick_mid[...], u2[...].reshape(512, 128)).astype(BF16).reshape(4, 128, 128)
@@ -423,30 +430,45 @@
     arrive(copies)
     heads[...] = dot(pick_out[...], u3[...].reshape(512, 128)).astype(BF16)
 
+    def half(e, t, h):
+        if last_axis[e] == "y":
+            return partial.at[e, pl.ds(2 * h, 2), t]
+        return partial.at[e, t, pl.ds(2 * h, 2)]
+
+    def ends_of(e):
+        here = getattr(me, last_axis[e])
+        return (
+            [(here + d) % 4 for d in range(4)],
+            me.at(**{last_axis[e]: 1}),
+            me.at(**{last_axis[e]: 3}),
+        )
+
     def send_rows(e):
-        copies = []
-        for d in (1, 2, 3):
-            if last_axis[e] == "y":
-                src = partial.at[e, :, (me.y + d) % 4]
-            else:
-                src = partial.at[e, (me.x + d) % 4]
-            copies.append(wire.send(src, ra.at[e, d - 1], me.at(**{last_axis[e]: d})))
-        return copies
+        t, up, down = ends_of(e)
+        relayed = [
+            wire.send(half(e, t[2], 0), ra.at[e, 0], up),
+            wire.send(half(e, t[2], 1), ra.at[e, 1], down),
+        ]
+        return relayed, [
+            wire.send(half(e, t[1], 1), ra.at[e, 2], up),
+            wire.send(half(e, t[3], 0), ra.at[e, 3], down),
+        ]
+
+    def relay_rows(e, relayed, direct):
+        t, up, down = ends_of(e)
+        arrive(relayed)
+        relay[e, 0] = (half(e, t[1], 0)[...].astype(F32) + ra[e, 0].astype(F32)).astype(BF16)
+        first = wire.send(relay.at[e, 0], ra.at[e, 4], up)
+        relay[e, 1] = (half(e, t[3], 1)[...].astype(F32) + ra[e, 1].astype(F32)).astype(BF16)
+        return direct + [first, wire.send(relay.at[e, 1], ra.at[e, 5], down)]
 
     def send_row(e, copies):
         arrive(copies)
-
-        def body(i, _):
-            if last_axis[e] == "y":
-                total = partial[e, i, me.y].astype(F32)
-            else:
-                total = partial[e, me.x, i].astype(F32)
-            for d in range(3):
-                total = total + ra[e, d, i].astype(F32)
-            sa[e, i] = total.astype(BF16)
-            return 0
-
-        lax.fori_loop(0, 4, body, 0)
+        here = getattr(me, last_axis[e])
+        for h, (a, b) in enumerate(((3, 4), (2, 5))):
+            total = half(e, here, h)[...].astype(F32)
+            total = total + ra[e, a].astype(F32) + ra[e, b].astype(F32)
+            sa[e, 2 * h : 2 * h + 2] = total.astype(BF16)
         here = getattr(me, first_axis[e])
         return [
             wire.send(sa.at[e, (here + d) % 4], rb.at[e, d - 1], me.at(**{first_axis[e]: d}))
@@ -466,13 +488,15 @@
 
     rows = {}
     out_products(0, early, heads, wo, partial)
-    rows[1] = send_rows(1)
-    rows[0] = send_rows(0)
+    for e in (1, 0):
+        rows[e] = send_rows(e)
     arrive([near[1]])
     down_products(1, blocks, wd, early)
     out_products(1, early, heads, wo, partial)
-    rows[2] = send_rows(2)
-    rows[3] = send_rows(3)
+    for e in (2, 3):
+        rows[e] = send_rows(e)
+    for e in (1, 0, 2, 3):
+        rows[e] = relay_rows(e, *rows[e])
     row = {1: send_row(1, rows[1])}
     row[0] = send_row(0, rows[0])
     row[2] = send_row(2, rows[2])
@@ -501,7 +525,7 @@
         ((8, 128), F32), ((8, 128), F32), ((8, 128), F32), ((2, 4, 8, 128), F32),
         ((4, 16, HALF), BF16), ((4, 4, 4, 16, HALF), BF16),
         ((512, WIDTH), BF16), ((4, 2, 2, 32, 128), BF16), ((4, 2, 2, 32, HALF), BF16),
-        ((2, 2, 2, 32, HALF), BF16), ((2, 2, 2, 32, HALF), BF16), ((2, 2, 32, HALF), BF16),
+        ((4, 2, 32, HALF), BF16), ((4, 2, 32, HALF), BF16), ((4, 32, HALF), BF16),
         ((4, 2, 2, 32, 640), BF16),
         ((2, 4, 2, 32, 128), BF16), ((2, 4, 32, 128), BF16), ((2, 4, 32, 128), BF16),
         ((4, 32, 128), BF16), ((4, 4, 32, 128), BF16), ((128, 128), F32), ((4, 32, 128), BF16),
@@ -509,7 +533,8 @@
         ((2, 4, 32, 128), BF16), ((4, 64, 128), BF16), ((2, 4, 64, 128), BF16),
         ((4, 128, 128), BF16), ((4, 128, 128), BF16), ((512, 128), BF16),
         ((128, 512), BF16), ((512, 512), BF16), ((512, 512), BF16),
-        ((256, WIDTH), F32), ((4, 4, 4, 16, HALF), BF16), ((4, 3, 4, 16, HALF), BF16), ((4, 4, 16, HALF), BF16),
+        ((256, WIDTH), F32), ((4, 4, 4, 16, HALF), BF16), ((4, 6, 2, 16, HALF), BF16),
+        ((4, 2, 2, 16, HALF), BF16), ((4, 4, 16, HALF), BF16),
         ((4, 3, 16, HALF), BF16), ((3, 16, HALF), BF16), ((3, 16, HALF), BF16),
         128, 128,
     ]
@@ -524,7 +549,7 @@
             for entry in scratch
         ],
         compiler_params=pltpu.CompilerParams(
-            collective_id=0, has_side_effects=True, vmem_limit_bytes=56 * 2**20
+            collective_id=0, has_side_effects=True, vmem_limit_bytes=56 * 2**20 - 160 * 2**10
         ),
     )(
         lengths, hidden_in, norm_gain, w_qkv.T, w_gate.T, w_up.T,

time: 103 us -> 97.8 us (0.950)
  Pallas kernels: 101 us -> 95.6 us
    pallas_call x1, Pallas kernels: 101 us -> 95.6 us  [per_device(): pl.pallas_call(kernel, name='layer', out_shape=jax.ShapeDtypeStruct((2, 4...]
where the time goes in v4:
time: 97.8 us; the launch traced here: 97.7 us
  Pallas kernels  95.6 us (98%)
  local copies, waits for them, and re-layouts  1.4 us (1%)
    pallas_call x1, Pallas kernels, per_device(): pl.pallas_call(kernel, name='layer', out_shape=jax.ShapeDtypeStruct((2, 4...  95.6 us

profile of v4, /device:TPU:2, one launch (start us, length us, event | category | flops | bytes accessed | tf_op | source)
XLA Modules:
  0.0 97.7 jit_solution(11607772706285423086)
XLA Ops:
  0.7 95.6 %layer.1 = bf16[2,4,2304]{2,1,0:T(4,128)(2,1)} custom-call(s32[1]{0:T(128)S(6)} %copy.11.lengths_ref, bf16[2,4,2304]{2,1,0:T(4,128)(2,1)} %hidden_hbm.1, f32[2304]{0:T(1024)} %gain_hbm.1, bf16[104,2304]{1,0:T(8,128)(2,1)} %bitcast.5, bf16[576,2304]{1,0:T(8,128)(2,1)} %bitcast.3, bf16[576,2304]{1,0:T(8,128)(2,1)} %bitcast.4, bf16[96,2304]{1,0:T(8,128)(2,1)} %wo_hbm.1, ...), custom_call_target="tpu_custom_call" | custom-call | tf_op jit(solution)/shard_map/layer/pallas_call | solution.py:541
  96.3 1.4 %copy.12 = bf16[2,4,2304]{2,1,0:T(4,128)(2,1)} copy(bf16[2,4,2304]{2,1,0:T(4,128)(2,1)} %layer.1) | data formatting | bytes 73728

commit v5 on v4

--- a/solution.py
+++ b/solution.py
@@ -495,16 +495,16 @@
     out_products(1, early, heads, wo, partial)
     for e in (2, 3):
         rows[e] = send_rows(e)
-    for e in (1, 0, 2, 3):
+    for e in (1, 2, 3, 0):
         rows[e] = relay_rows(e, *rows[e])
     row = {1: send_row(1, rows[1])}
-    row[0] = send_row(0, rows[0])
     row[2] = send_row(2, rows[2])
     ends = [send_block(1, row[1])]
     row[3] = send_row(3, rows[3])
+    row[0] = send_row(0, rows[0])
     ends.append(send_block(2, row[2]))
+    ends.append(send_block(3, row[3]))
     total = row_sum(0, row[0])
-    ends.append(send_block(3, row[3]))
     arrive(ends)
     for e in range(3):
         total = total + rz[e].astype(F32)

time: 97.8 us -> 97.4 us (level)
  no operation moved by 1% of the time
where the time goes in v5:
time: 97.4 us; the launch traced here: 96.8 us
  Pallas kernels  94.7 us (97%)
  local copies, waits for them, and re-layouts  1.4 us (1%)
    pallas_call x1, Pallas kernels, per_device(): pl.pallas_call(kernel, name='layer', out_shape=jax.ShapeDtypeStruct((2, 4...  94.7 us

profile of v5, /device:TPU:2, one launch (start us, length us, event | category | flops | bytes accessed | tf_op | source)
XLA Modules:
  0.0 96.8 jit_solution(27854646496784028)
XLA Ops:
  0.7 94.7 %layer.1 = bf16[2,4,2304]{2,1,0:T(4,128)(2,1)} custom-call(s32[1]{0:T(128)S(6)} %copy.11.lengths_ref, bf16[2,4,2304]{2,1,0:T(4,128)(2,1)} %hidden_hbm.1, f32[2304]{0:T(1024)} %gain_hbm.1, bf16[104,2304]{1,0:T(8,128)(2,1)} %bitcast.5, bf16[576,2304]{1,0:T(8,128)(2,1)} %bitcast.3, bf16[576,2304]{1,0:T(8,128)(2,1)} %bitcast.4, bf16[96,2304]{1,0:T(8,128)(2,1)} %wo_hbm.1, ...), custom_call_target="tpu_custom_call" | custom-call | tf_op jit(solution)/shard_map/layer/pallas_call | solution.py:541
  95.4 1.4 %copy.12 = bf16[2,4,2304]{2,1,0:T(4,128)(2,1)} copy(bf16[2,4,2304]{2,1,0:T(4,128)(2,1)} %layer.1) | data formatting | bytes 73728
